TPU v7x, 512 devices: a whole 4x4x16 slice. The times are simulated.
512 devices in a mesh: hst: 64 (over y, z_lo, core), head: 8 (over x, z_hi).
Axes of the slice: x: 4, y: 4, z: 16 (z_hi: 2, z_lo: 8; z = z_hi * 8 + z_lo), core: 2. Of those that a mesh axis runs over, the one named last changes fastest.
Arguments:
- queries: bfloat16 [16384, 4096], P('hst', 'head')
- keys: bfloat16 [16384, 1024], P('hst', 'head')
- values: bfloat16 [16384, 1024], P('hst', 'head'), may hold values from -24 to 24
- passing_index: int32 [64, 128], P('hst'), may hold values from 0 to 255, as said below
- out_weight: bfloat16 [4096, 4096], P('head'), may hold values from -0.09375 to 0.09375
Outputs:
- mixed: bfloat16 [16384, 4096], P('hst', 'head')
Inputs may be any that keep to these rules, and one draw needn't show every extreme that they name: `passing_index`: each shard's 128 positions are distinct.
All inputs are finite; a program needn't handle non-finite values.
Results may differ from a plain program's by a relative error of at most 0.019.
Values may be sent and summed in bfloat16 or wider, within the bound.
No kernel may reach another device: no remote copies, remote signals or barrier semaphores. Data moves between devices by JAX's collectives and lax.ppermute only.
A program may use at most 64 MiB of HBM per device.

v0:
```python
import math

import jax
import jax.numpy as jnp
from jax import lax
from jax.experimental import pallas as pl
from jax.experimental.pallas import tpu as pltpu
from jax.sharding import PartitionSpec as P

HD = 128
PASS = 128
ANCHOR = 128
GROUPS = 4
ROWS = 256
HALF = ROWS // 2
QROWS = ROWS * GROUPS
HROWS = HALF * GROUPS
TILE = 512
SCALE = math.log2(math.e) / math.sqrt(HD)
LOW = -1e30
BF = jnp.bfloat16
F32 = jnp.float32
VM = pl.BlockSpec(memory_space=pltpu.VMEM)
SM = pl.BlockSpec(memory_space=pltpu.SMEM)
HBM = pl.BlockSpec(memory_space=pltpu.HBM)


def dot_nt(a, b):
    return lax.dot_general(a, b, (((1,), (1,)), ((), ())), preferred_element_type=F32)


def fetch(pairs, sems):
    copies = [pltpu.make_async_copy(a, b, sems.at[i]) for i, (a, b) in enumerate(pairs)]
    for copy in copies:
        copy.start()
    return copies


def wait(copies):
    for copy in copies:
        copy.wait()


def prepare(place_ref, index_hbm, key_hbm, value_hbm, passed_ref, anchor_ref, index_ref, both_ref, sems):
    wait(
        fetch(
            [(index_hbm, index_ref), (key_hbm, both_ref.at[:, :HD]), (value_hbm, both_ref.at[:, HD:])],
            sems,
        )
    )
    rows = lax.broadcasted_iota(jnp.int32, (ROWS, PASS), 0)
    pick = jnp.where(rows == index_ref[...], 1.0, 0.0).astype(BF)
    both = both_ref[...]
    passed_ref[...] = lax.dot_general(
        pick, both, (((0,), (0,)), ((), ())), preferred_element_type=F32
    ).astype(BF)
    anchor_ref[...] = jnp.where(place_ref[0] == 0, both[:ANCHOR], jnp.zeros_like(both[:ANCHOR]))


def pack_far(pieces_hbm, anchor_hbm, out_hbm, held_ref, sems):
    size = pieces_hbm.shape[0]
    wait(fetch([(pieces_hbm, held_ref.at[:size]), (anchor_hbm, held_ref.at[size:])], sems))
    wait(fetch([(held_ref, out_hbm.at[y]) for y in range(4)], sems))


def position(place_ref):
    me = place_ref[0]
    return me // 16, lax.rem(me // 2, 8), lax.rem(me, 2)


def tile(scaled_ref, acc_ref, top_ref, start, key, value, mask, first):
    span = slice(start, start + TILE)
    s = dot_nt(scaled_ref[span], key)
    if mask is not None:
        s = jnp.where(mask, s, LOW)
    parts = [s[:, j * HD : (j + 1) * HD] for j in range(s.shape[1] // HD)]
    high = parts[0]
    for part in parts[1:]:
        high = jnp.maximum(high, part)
    high = jnp.max(high, axis=1, keepdims=True)
    if first:
        new = jnp.broadcast_to(high, (TILE, HD))
    else:
        old = top_ref[span]
        new = jnp.maximum(old, high)
    weights = jnp.concatenate([jnp.exp2(part - new).astype(BF) for part in parts], axis=1)
    total = jnp.dot(weights, value, preferred_element_type=F32)
    if not first:
        shrink = jnp.exp2(old - new)
        total = acc_ref[span] * jnp.concatenate([shrink, shrink], axis=1) + total
    acc_ref[span] = total
    top_ref[span] = new


def attend(scaled_ref, acc_ref, top_ref, block, mask=None, first=False):
    keys, count = block[:, :HD], block.shape[0]
    key = jnp.concatenate([keys, keys], axis=1)
    value = jnp.concatenate([block[:, HD:], jnp.ones((count, HD), BF)], axis=1)
    for number in range(QROWS // TILE):
        one = mask(number) if mask is not None else None
        tile(scaled_ref, acc_ref, top_ref, number * TILE, key, value, one, first)


def own_tokens(query_ref, local_ref, scaled_ref, acc_ref, top_ref):
    for half in range(2):
        for g in range(GROUPS):
            part = query_ref[half * HALF : (half + 1) * HALF, g * HD : (g + 1) * HD].astype(F32) * SCALE
            high = part.astype(BF)
            low = (part - high.astype(F32)).astype(BF)
            start = half * HROWS + g * HALF
            scaled_ref[start : start + HALF, :] = jnp.concatenate([high, low], axis=1)
    token = lax.broadcasted_iota(jnp.int32, (TILE, ROWS), 0) % HALF
    key = lax.broadcasted_iota(jnp.int32, (TILE, ROWS), 1)

    def causal(number):
        return key <= token + (number * TILE // HROWS) * HALF

    attend(scaled_ref, acc_ref, top_ref, local_ref[...], causal, first=True)


NEAR = (0, 4, 2, 6)
FAR = (1, 5, 3, 7)


def visit(place_ref, scaled_ref, acc_ref, top_ref, pieces_ref, spots):
    y, z, c = position(place_ref)
    count = len(spots) * PASS
    lane = lax.broadcasted_iota(jnp.int32, (1, count), 1) // PASS

    @pl.loop(0, y + 1)
    def _(row):
        for side in range(2):
            core = c if side == 0 else 1 - c
            seen = jnp.zeros((1, count), jnp.int32)
            for spot, k in enumerate(spots):
                before = lax.rem(z // (1 << (k.bit_length() - 1)), 2) == 1 if k else core < c
                seen = jnp.where(lane == spot, (before | (row < y)).astype(jnp.int32), seen)
            attend(scaled_ref, acc_ref, top_ref, pieces_ref[side, row, :count], lambda number: seen > 0)


def visit_anchor(place_ref, scaled_ref, acc_ref, top_ref, pieces_ref):
    me = place_ref[0]

    @pl.when(me > 0)
    def _():
        attend(scaled_ref, acc_ref, top_ref, pieces_ref[lax.rem(me, 2), 0, 4 * PASS :])


def attend_near(
    place_ref, query_hbm, key_hbm, value_hbm, ours_hbm, theirs_hbm, scaled_hbm, acc_hbm, top_hbm,
    query_ref, local_ref, pieces_ref, scaled_ref, acc_ref, top_ref, sems,
):
    copies = fetch(
        [
            (query_hbm, query_ref),
            (key_hbm, local_ref.at[:, :HD]),
            (value_hbm, local_ref.at[:, HD:]),
            (ours_hbm, pieces_ref.at[0]),
            (theirs_hbm, pieces_ref.at[1]),
        ],
        sems,
    )
    wait(copies[:3])
    own_tokens(query_ref, local_ref, scaled_ref, acc_ref, top_ref)
    wait(copies[3:])
    visit(place_ref, scaled_ref, acc_ref, top_ref, pieces_ref, NEAR)
    wait(fetch([(scaled_ref, scaled_hbm), (acc_ref, acc_hbm), (top_ref, top_hbm)], sems))


def attend_far(
    place_ref, scaled_hbm, acc_hbm, top_hbm, ours_hbm, theirs_hbm, weight_hbm, away_hbm, attended_hbm,
    out_ref, attended_ref, weight_ref, pieces_ref, scaled_ref, acc_ref, top_ref, sems,
):
    copies = fetch(
        [
            (scaled_hbm, scaled_ref),
            (acc_hbm, acc_ref),
            (top_hbm, top_ref),
            (ours_hbm, pieces_ref.at[0]),
            (theirs_hbm, pieces_ref.at[1]),
            (weight_hbm, weight_ref),
        ],
        sems,
    )
    wait(copies[:5])
    visit(place_ref, scaled_ref, acc_ref, top_ref, pieces_ref, FAR)
    visit_anchor(place_ref, scaled_ref, acc_ref, top_ref, pieces_ref)
    result = (acc_ref[:, :HD] / acc_ref[:, HD:]).astype(BF)
    attended = jnp.concatenate(
        [
            jnp.concatenate(
                [result[half * HROWS + g * HALF : half * HROWS + (g + 1) * HALF] for g in range(GROUPS)], axis=1
            )
            for half in range(2)
        ],
        axis=0,
    )
    attended_ref[...] = attended
    sent = [pltpu.make_async_copy(attended_ref, attended_hbm, sems.at[0])]
    sent[0].start()
    wait(copies[5:])
    project(attended, weight_ref, 1 - lax.rem(place_ref[1], 2), out_ref)
    wait(sent + fetch([(out_ref, away_hbm)], sems.at[1:]))


def project(rows, weight_ref, side, out_ref):
    width = out_ref.shape[2]
    for x in range(4):
        columns = pl.ds(pl.multiple_of((2 * x + side) * width, width), width)
        out_ref[x] = jnp.dot(rows, weight_ref[:, columns], preferred_element_type=F32).astype(BF)


def project_home(place_ref, rows_hbm, weight_hbm, home_hbm, out_ref, rows_ref, weight_ref, sems):
    wait(fetch([(rows_hbm, rows_ref), (weight_hbm, weight_ref)], sems))
    project(rows_ref[...], weight_ref, lax.rem(place_ref[1], 2), out_ref)
    wait(fetch([(out_ref, home_hbm)], sems))


def widen(value_ref, out_ref):
    out_ref[...] = value_ref[...].astype(F32)


def add_up(other_ref, parts_ref, out_ref):
    total = other_ref[...]
    for x in range(4):
        total = total + parts_ref[x].astype(F32)
    out_ref[...] = total.astype(BF)


def shape(*dims, dtype=BF):
    return jax.ShapeDtypeStruct(dims, dtype)


def shards(queries, keys, values, passing_index, out_weight):
    me = lax.axis_index("hst")
    head = lax.axis_index("head")

    def over_z(value, k):
        return lax.ppermute(value, "hst", [(i, i ^ (2 * k)) for i in range(64)])

    def over_core(value):
        return lax.ppermute(value, "hst", [(i, i ^ 1) for i in range(64)])

    def four(value):
        return jnp.broadcast_to(value[None], (4,) + value.shape)

    def over_y(value):
        groups = [[16 * row + i for row in range(4)] for i in range(16)]
        return lax.all_to_all(value, "hst", 0, 0, axis_index_groups=groups)

    place = jnp.stack([me, head]).astype(jnp.int32)

    def call(kernel, out_shape, in_specs, out_specs, *args, scratch=(), limit=int(63.75 * 2**20), flops=2**20):
        return pl.pallas_call(
            kernel,
            out_shape=out_shape,
            in_specs=in_specs,
            out_specs=out_specs,
            scratch_shapes=scratch,
            compiler_params=pltpu.CompilerParams(vmem_limit_bytes=limit),
            cost_estimate=pl.CostEstimate(flops=flops, bytes_accessed=2**16, transcendentals=0),
        )(*args)

    def spread(value, k):
        step = 2 * k
        return value + lax.ppermute(value, "hst", [(i, i + step) for i in range(0, 16, 2 * step)])

    def over_x(value):
        return lax.all_to_all(value, "head", 0, 0, axis_index_groups=[[0, 2, 4, 6], [1, 3, 5, 7]])

    copies = pltpu.SemaphoreType.DMA((6,))
    passed, anchor = call(
        prepare,
        (shape(PASS, 2 * HD), shape(ANCHOR, 2 * HD)),
        [SM] + [HBM] * 3,
        (VM,) * 2,
        place,
        passing_index,
        keys,
        values,
        scratch=[pltpu.VMEM((1, PASS), jnp.int32), pltpu.VMEM((ROWS, 2 * HD), BF), copies],
    )

    mirror, anchor = over_z(passed, 4), spread(anchor, 4)
    mirror, anchor = lax.optimization_barrier((mirror, anchor))
    two = jnp.concatenate([passed, mirror], axis=0)
    pair, anchor = lax.optimization_barrier((over_z(two, 2), spread(anchor, 2)))
    near = jnp.concatenate([two, pair], axis=0)
    far = call(
        pack_far,
        shape(4, 5 * PASS, 2 * HD),
        [HBM] * 2,
        HBM,
        over_z(near, 1),
        spread(anchor, 1),
        scratch=[pltpu.VMEM((5 * PASS, 2 * HD), BF), copies],
        flops=2 * 10**9,
    )

    near_y, far = lax.optimization_barrier((over_y(four(near)), far))
    far_y = over_y(far)
    width = GROUPS * HD
    state = [
        pltpu.VMEM((QROWS, 2 * HD), BF),
        pltpu.VMEM((QROWS, 2 * HD), F32),
        pltpu.VMEM((QROWS, HD), F32),
        copies,
    ]
    scaled, acc, top = call(
        attend_near,
        (shape(QROWS, 2 * HD), shape(QROWS, 2 * HD, dtype=F32), shape(QROWS, HD, dtype=F32)),
        [SM] + [HBM] * 5,
        (HBM,) * 3,
        place,
        queries,
        keys,
        values,
        near_y,
        over_core(near_y),
        scratch=[pltpu.VMEM((ROWS, width), BF), pltpu.VMEM((ROWS, 2 * HD), BF)]
        + [pltpu.VMEM((2,) + near_y.shape, BF)]
        + state,
    )
    far_y, acc, top = lax.optimization_barrier((far_y, acc, top))
    away, attended = call(
        attend_far,
        (shape(4, ROWS, width), shape(ROWS, width)),
        [SM] + [HBM] * 6,
        (HBM,) * 2,
        place,
        scaled,
        acc,
        top,
        far_y,
        over_core(far_y),
        out_weight,
        scratch=[pltpu.VMEM((4, ROWS, width), BF), pltpu.VMEM((ROWS, width), BF), pltpu.VMEM(out_weight.shape, BF)]
        + [pltpu.VMEM((2,) + far_y.shape, BF)]
        + state,
    )

    home = call(
        project_home,
        shape(4, ROWS, width),
        [SM] + [HBM] * 2,
        HBM,
        place,
        attended,
        out_weight,
        scratch=[
            pltpu.VMEM((4, ROWS, width), BF),
            pltpu.VMEM((ROWS, width), BF),
            pltpu.VMEM(out_weight.shape, BF),
            copies,
        ],
        flops=10**10,
    )
    away, home = lax.optimization_barrier((over_x(away), home))
    other = jnp.sum(away.astype(F32), axis=0).astype(BF)
    other = lax.ppermute(other, "head", [(i, i ^ 1) for i in range(8)])
    parts = over_x(home)
    return call(
        add_up,
        shape(ROWS, width),
        [VM] * 2,
        VM,
        call(widen, shape(ROWS, width, dtype=F32), [VM], VM, other, limit=2**24, flops=10**11),
        parts,
        limit=2**24,
    )


def solution(mesh):
    in_specs = (
        P("hst", "head"),
        P("hst", "head"),
        P("hst", "head"),
        P("hst", None),
        P("head", None),
    )
    out_specs = P("hst", "head")
    return jax.shard_map(shards, mesh=mesh, in_specs=in_specs, out_specs=out_specs, check_vma=False)
```

profile of v0, /device:TPU:1, one launch (start us, length us, event | category | flops | bytes accessed | tf_op | source)
XLA Modules:
  0.0 147.8 jit_solution(8819472981190548572)
XLA Ops:
  0.0 0.6 pad_add_fusion.place_ref
  0.6 2.4 %shard_map.55 = (bf16[128,256]{1,0:T(8,128)(2,1)}, bf16[128,256]{1,0:T(8,128)(2,1)}) custom-call(s32[2]{0:T(128)} %pad_add_fusion.place_ref, s32[1,128]{1,0:T(1,128)} %index_hbm.1, bf16[256,128]{1,0:T(8,128)(2,1)} %key_hbm.3, bf16[256,128]{1,0:T(8,128)(2,1)} %value_hbm.3), custom_call_target="tpu_custom_call" | custom-call | flops 1048576 | bytes 65536 | tf_op jit(solution)/shard_map/pallas_call | solution.py:254
  3.0 0.7 collective-permute-start.1
  3.7 9.6 %collective-permute-start = (bf16[128,256]{1,0:T(8,128)(2,1)}, bf16[128,256]{1,0:T(8,128)(2,1)S(1)}, u32[]{:S(2)}, u32[]{:S(2)}) collective-permute-start(bf16[128,256]{1,0:T(8,128)(2,1)} %get-tuple-element.23), channel_id=1, source_target_pairs={{0,64},{8,72},{16,80},{24,88},{32,96},{40,104},{48,112},{56,120},{... | collective-permute-start | bytes 196616 | tf_op jit(solution)/shard_map/ppermute | solution.py:239
  13.4 0.0 collective-permute-done.1
  13.4 0.9 add.9
  14.2 1.0 collective-permute-done
  15.2 0.8 pad_maximum_fusion
  16.1 7.8 %collective-permute-start.2 = (bf16[256,256]{1,0:T(8,128)(2,1)S(1)}, bf16[256,256]{1,0:T(8,128)(2,1)S(1)}, u32[]{:S(2)}, u32[]{:S(2)}) collective-permute-start(bf16[256,256]{1,0:T(8,128)(2,1)S(1)} %pad_maximum_fusion), channel_id=1, source_target_pairs={{0,32},{8,40},{16,48},{24,56},{32,0},{40,8},{48,16},{56,24},{64,96... | collective-permute-start | bytes 393224 | tf_op jit(solution)/shard_map/ppermute | solution.py:239
  23.9 0.8 constant_dynamic-update-slice_fusion.2
  24.7 0.7 collective-permute-start.3
  25.4 0.0 collective-permute-done.3
  25.4 0.8 collective-permute-done.2
  26.2 1.0 broadcast_in_dim.2
  27.3 4.3 %all-to-all-start = ((bf16[4,512,256]{2,1,0:T(8,128)(2,1)}), bf16[4,512,256]{2,1,0:T(8,128)(2,1)}, u32[]{:S(2)}, u32[]{:S(2)}) async-start(bf16[4,512,256]{2,1,0:T(8,128)(2,1)} %broadcast_in_dim.2), calls=%async_computation | async-start | bytes 2097152 | tf_op jit(solution)/shard_map/all_to_all | solution.py:249
  31.5 5.9 %collective-permute-start.4 = (bf16[512,256]{1,0:T(8,128)(2,1)S(1)}, bf16[512,256]{1,0:T(8,128)(2,1)}, u32[]{:S(2)}, u32[]{:S(2)}) collective-permute-start(bf16[512,256]{1,0:T(8,128)(2,1)S(1)} %constant_dynamic-update-slice_fusion), channel_id=1, source_target_pairs={{0,16},{8,24},{16,0},{24,8},{32,48},{40,56},{48,32},{56,40},{64,80... | collective-permute-start | bytes 786440 | tf_op jit(solution)/shard_map/ppermute | solution.py:239
  37.5 0.7 collective-permute-start.5
  38.2 0.0 collective-permute-done.5
  38.2 0.6 add.11.anchor_hbm
  38.8 2.5 %collective-permute-done.4.pieces_hbm = bf16[512,256]{1,0:T(8,128)(2,1)} collective-permute-done((bf16[512,256]{1,0:T(8,128)(2,1)S(1)}, bf16[512,256]{1,0:T(8,128)(2,1)}, u32[]{:S(2)}, u32[]{:S(2)}) %collective-permute-start.4) | collective-permute-done | bytes 262176 | tf_op jit(solution)/shard_map/ppermute | solution.py:239
  41.4 2.1 %shard_map.56 = bf16[4,640,256]{2,1,0:T(8,128)(2,1)} custom-call(bf16[512,256]{1,0:T(8,128)(2,1)} %collective-permute-done.4.pieces_hbm, bf16[128,256]{1,0:T(8,128)(2,1)} %add.11.anchor_hbm), custom_call_target="tpu_custom_call" | custom-call | flops 2000000000 | bytes 65536 | tf_op jit(solution)/shard_map/pallas_call | solution.py:254
  43.4 0.0 all-to-all-done.ours_hbm
  43.5 9.0 %collective-permute-start.6 = (bf16[4,512,256]{2,1,0:T(8,128)(2,1)}, bf16[4,512,256]{2,1,0:T(8,128)(2,1)}, u32[]{:S(2)}, u32[]{:S(2)}) collective-permute-start(bf16[4,512,256]{2,1,0:T(8,128)(2,1)} %all-to-all-done.ours_hbm), channel_id=1, source_target_pairs={{0,8},{8,0},{16,24},{24,16},{32,40},{40,32},{48,56},{56,48},{64,72... | collective-permute-start | bytes 3145736 | tf_op jit(solution)/shard_map/ppermute | solution.py:242
  52.5 4.3 %all-to-all-start.1 = ((bf16[4,640,256]{2,1,0:T(8,128)(2,1)}), bf16[4,640,256]{2,1,0:T(8,128)(2,1)}, u32[]{:S(2)}, u32[]{:S(2)}) async-start(bf16[4,640,256]{2,1,0:T(8,128)(2,1)} %shard_map.56), calls=%async_computation.1 | async-start | bytes 2621440 | tf_op jit(solution)/shard_map/all_to_all | solution.py:249
  56.8 0.0 collective-permute-done.6.theirs_hbm
  56.8 5.5 %shard_map.57 = (bf16[1024,256]{1,0:T(8,128)(2,1)}, f32[1024,256]{1,0:T(8,128)}, f32[1024,128]{1,0:T(8,128)}) custom-call(s32[2]{0:T(128)} %pad_add_fusion.place_ref, bf16[256,512]{1,0:T(8,128)(2,1)} %query_hbm.1, bf16[256,128]{1,0:T(8,128)(2,1)} %key_hbm.3, bf16[256,128]{1,0:T(8,128)(2,1)} %value_hbm.3, bf16[4,512,256]{2,1,0:T(8,128)(2,1)} %all-to-all-done.ours_hbm, ...), custom_call_target="tpu_custom_call" | custom-call | flops 1048576 | bytes 65536 | tf_op jit(solution)/shard_map/pallas_call | solution.py:254
  62.3 12.6 %all-to-all-done.1.ours_hbm = bf16[4,640,256]{2,1,0:T(8,128)(2,1)} async-done(((bf16[4,640,256]{2,1,0:T(8,128)(2,1)}), bf16[4,640,256]{2,1,0:T(8,128)(2,1)}, u32[]{:S(2)}, u32[]{:S(2)}) %all-to-all-start.1) | async-done | bytes 1310752 | tf_op jit(solution)/shard_map/all_to_all | solution.py:249
  74.9 2.7 %collective-permute-start.7 = (bf16[4,640,256]{2,1,0:T(8,128)(2,1)}, bf16[4,640,256]{2,1,0:T(8,128)(2,1)}, u32[]{:S(2)}, u32[]{:S(2)}) collective-permute-start(bf16[4,640,256]{2,1,0:T(8,128)(2,1)} %all-to-all-done.1.ours_hbm), channel_id=1, source_target_pairs={{0,8},{8,0},{16,24},{24,16},{32,40},{40,32},{48,56},{56,48},{64,72... | collective-permute-start | bytes 3932168 | tf_op jit(solution)/shard_map/ppermute | solution.py:242
  77.6 3.0 %collective-permute-done.7.theirs_hbm = bf16[4,640,256]{2,1,0:T(8,128)(2,1)} collective-permute-done((bf16[4,640,256]{2,1,0:T(8,128)(2,1)}, bf16[4,640,256]{2,1,0:T(8,128)(2,1)}, u32[]{:S(2)}, u32[]{:S(2)}) %collective-permute-start.7) | collective-permute-done | bytes 1310752 | tf_op jit(solution)/shard_map/ppermute | solution.py:242
  80.6 7.3 %shard_map.58 = (bf16[4,256,512]{2,1,0:T(8,128)(2,1)}, bf16[256,512]{1,0:T(8,128)(2,1)}) custom-call(s32[2]{0:T(128)} %pad_add_fusion.place_ref, bf16[1024,256]{1,0:T(8,128)(2,1)} %get-tuple-element.30.scaled_hbm, f32[1024,256]{1,0:T(8,128)} %get-tuple-element.34.acc_hbm, f32[1024,128]{1,0:T(8,128)} %get-tuple-element.35.top_hbm, ...), custom_call_target="tpu_custom_call" | custom-call | flops 1048576 | bytes 65536 | tf_op jit(solution)/shard_map/pallas_call | solution.py:254
  87.9 4.2 %all-to-all-start.2 = ((bf16[4,256,512]{2,1,0:T(8,128)(2,1)}), bf16[4,256,512]{2,1,0:T(8,128)(2,1)}, u32[]{:S(2)}, u32[]{:S(2)}) async-start(bf16[4,256,512]{2,1,0:T(8,128)(2,1)} %get-tuple-element.37), calls=%async_computation.2 | async-start | bytes 2097152 | tf_op jit(solution)/shard_map/all_to_all | solution.py:269
  92.2 4.7 %shard_map.59 = bf16[4,256,512]{2,1,0:T(8,128)(2,1)} custom-call(s32[2]{0:T(128)} %pad_add_fusion.place_ref, bf16[256,512]{1,0:T(8,128)(2,1)} %get-tuple-element.38.rows_hbm, bf16[512,4096]{1,0:T(8,128)(2,1)} %weight_hbm.3), custom_call_target="tpu_custom_call" | custom-call | flops 10000000000 | bytes 65536 | tf_op jit(solution)/shard_map/pallas_call | solution.py:254
  96.9 10.9 %all-to-all-done.2 = bf16[4,256,512]{2,1,0:T(8,128)(2,1)} async-done(((bf16[4,256,512]{2,1,0:T(8,128)(2,1)}), bf16[4,256,512]{2,1,0:T(8,128)(2,1)}, u32[]{:S(2)}, u32[]{:S(2)}) %all-to-all-start.2) | async-done | bytes 1048608 | tf_op jit(solution)/shard_map/all_to_all | solution.py:269
  107.8 1.5 reduce_sum.12
  109.2 15.6 %collective-permute-start.8 = (bf16[256,512]{1,0:T(8,128)(2,1)S(1)}, bf16[256,512]{1,0:T(8,128)(2,1)S(1)}, u32[]{:S(2)}, u32[]{:S(2)}) collective-permute-start(bf16[256,512]{1,0:T(8,128)(2,1)S(1)} %reduce_sum.12), channel_id=1, source_target_pairs={{0,1},{1,0},{2,3},{3,2},{4,5},{5,4},{6,7},{7,6},{8,9},{9,8},{10,11... | collective-permute-start | bytes 786440 | tf_op jit(solution)/shard_map/ppermute | solution.py:360
  124.8 3.5 %all-to-all-start.3 = ((bf16[4,256,512]{2,1,0:T(8,128)(2,1)}), bf16[4,256,512]{2,1,0:T(8,128)(2,1)S(1)}, u32[]{:S(2)}, u32[]{:S(2)}) async-start(bf16[4,256,512]{2,1,0:T(8,128)(2,1)} %shard_map.59), calls=%async_computation.3 | async-start | bytes 2097152 | tf_op jit(solution)/shard_map/all_to_all | solution.py:269
  128.4 18.5 %collective-permute-done.8.value_ref = bf16[256,512]{1,0:T(8,128)(2,1)S(1)} collective-permute-done((bf16[256,512]{1,0:T(8,128)(2,1)S(1)}, bf16[256,512]{1,0:T(8,128)(2,1)S(1)}, u32[]{:S(2)}, u32[]{:S(2)}) %collective-permute-start.8) | collective-permute-done | bytes 262176 | tf_op jit(solution)/shard_map/ppermute | solution.py:360
  146.9 0.0 all-to-all-done.3.parts_ref
  146.9 0.9 shard_map.61
  (4 shorter events, 0.1 us)
Async XLA Ops:
  3.0 10.3 %collective-permute-start.1 = (bf16[128,256]{1,0:T(8,128)(2,1)}, bf16[128,256]{1,0:T(8,128)(2,1)S(1)}, u32[]{:S(2)}, u32[]{:S(2)}) collective-permute-start(bf16[128,256]{1,0:T(8,128)(2,1)} %get-tuple-element.24), channel_id=1, source_target_pairs={{0,64},{1,65},{2,66},{3,67},{4,68},{5,69},{6,70},{7,71}} | collective-permute-start | bytes 196616 | tf_op jit(solution)/shard_map/ppermute | solution.py:266
  3.7 11.5 %collective-permute-start = (bf16[128,256]{1,0:T(8,128)(2,1)}, bf16[128,256]{1,0:T(8,128)(2,1)S(1)}, u32[]{:S(2)}, u32[]{:S(2)}) collective-permute-start(bf16[128,256]{1,0:T(8,128)(2,1)} %get-tuple-element.23), channel_id=1, source_target_pairs={{0,64},{8,72},{16,80},{24,88},{32,96},{40,104},{48,112},{56,120},{... | collective-permute-start | bytes 196616 | tf_op jit(solution)/shard_map/ppermute | solution.py:239
  16.1 10.2 %collective-permute-start.2 = (bf16[256,256]{1,0:T(8,128)(2,1)S(1)}, bf16[256,256]{1,0:T(8,128)(2,1)S(1)}, u32[]{:S(2)}, u32[]{:S(2)}) collective-permute-start(bf16[256,256]{1,0:T(8,128)(2,1)S(1)} %pad_maximum_fusion), channel_id=1, source_target_pairs={{0,32},{8,40},{16,48},{24,56},{32,0},{40,8},{48,16},{56,24},{64,96... | collective-permute-start | bytes 393224 | tf_op jit(solution)/shard_map/ppermute | solution.py:239
  24.7 0.7 collective-permute-start.3
  27.3 16.2 %all-to-all-start = ((bf16[4,512,256]{2,1,0:T(8,128)(2,1)}), bf16[4,512,256]{2,1,0:T(8,128)(2,1)}, u32[]{:S(2)}, u32[]{:S(2)}) async-start(bf16[4,512,256]{2,1,0:T(8,128)(2,1)} %broadcast_in_dim.2), calls=%async_computation | async-start | bytes 2097152 | tf_op jit(solution)/shard_map/all_to_all | solution.py:249
  31.5 9.8 %collective-permute-start.4 = (bf16[512,256]{1,0:T(8,128)(2,1)S(1)}, bf16[512,256]{1,0:T(8,128)(2,1)}, u32[]{:S(2)}, u32[]{:S(2)}) collective-permute-start(bf16[512,256]{1,0:T(8,128)(2,1)S(1)} %constant_dynamic-update-slice_fusion), channel_id=1, source_target_pairs={{0,16},{8,24},{16,0},{24,8},{32,48},{40,56},{48,32},{56,40},{64,80... | collective-permute-start | bytes 786440 | tf_op jit(solution)/shard_map/ppermute | solution.py:239
  37.5 0.7 collective-permute-start.5
  43.5 13.3 %collective-permute-start.6 = (bf16[4,512,256]{2,1,0:T(8,128)(2,1)}, bf16[4,512,256]{2,1,0:T(8,128)(2,1)}, u32[]{:S(2)}, u32[]{:S(2)}) collective-permute-start(bf16[4,512,256]{2,1,0:T(8,128)(2,1)} %all-to-all-done.ours_hbm), channel_id=1, source_target_pairs={{0,8},{8,0},{16,24},{24,16},{32,40},{40,32},{48,56},{56,48},{64,72... | collective-permute-start | bytes 3145736 | tf_op jit(solution)/shard_map/ppermute | solution.py:242
  52.5 22.4 %all-to-all-start.1 = ((bf16[4,640,256]{2,1,0:T(8,128)(2,1)}), bf16[4,640,256]{2,1,0:T(8,128)(2,1)}, u32[]{:S(2)}, u32[]{:S(2)}) async-start(bf16[4,640,256]{2,1,0:T(8,128)(2,1)} %shard_map.56), calls=%async_computation.1 | async-start | bytes 2621440 | tf_op jit(solution)/shard_map/all_to_all | solution.py:249
  74.9 5.7 %collective-permute-start.7 = (bf16[4,640,256]{2,1,0:T(8,128)(2,1)}, bf16[4,640,256]{2,1,0:T(8,128)(2,1)}, u32[]{:S(2)}, u32[]{:S(2)}) collective-permute-start(bf16[4,640,256]{2,1,0:T(8,128)(2,1)} %all-to-all-done.1.ours_hbm), channel_id=1, source_target_pairs={{0,8},{8,0},{16,24},{24,16},{32,40},{40,32},{48,56},{56,48},{64,72... | collective-permute-start | bytes 3932168 | tf_op jit(solution)/shard_map/ppermute | solution.py:242
  87.9 19.9 %all-to-all-start.2 = ((bf16[4,256,512]{2,1,0:T(8,128)(2,1)}), bf16[4,256,512]{2,1,0:T(8,128)(2,1)}, u32[]{:S(2)}, u32[]{:S(2)}) async-start(bf16[4,256,512]{2,1,0:T(8,128)(2,1)} %get-tuple-element.37), calls=%async_computation.2 | async-start | bytes 2097152 | tf_op jit(solution)/shard_map/all_to_all | solution.py:269
  109.2 37.6 %collective-permute-start.8 = (bf16[256,512]{1,0:T(8,128)(2,1)S(1)}, bf16[256,512]{1,0:T(8,128)(2,1)S(1)}, u32[]{:S(2)}, u32[]{:S(2)}) collective-permute-start(bf16[256,512]{1,0:T(8,128)(2,1)S(1)} %reduce_sum.12), channel_id=1, source_target_pairs={{0,1},{1,0},{2,3},{3,2},{4,5},{5,4},{6,7},{7,6},{8,9},{9,8},{10,11... | collective-permute-start | bytes 786440 | tf_op jit(solution)/shard_map/ppermute | solution.py:360
  124.8 22.1 %all-to-all-start.3 = ((bf16[4,256,512]{2,1,0:T(8,128)(2,1)}), bf16[4,256,512]{2,1,0:T(8,128)(2,1)S(1)}, u32[]{:S(2)}, u32[]{:S(2)}) async-start(bf16[4,256,512]{2,1,0:T(8,128)(2,1)} %shard_map.59), calls=%async_computation.3 | async-start | bytes 2097152 | tf_op jit(solution)/shard_map/all_to_all | solution.py:269
where the time goes:
time: 149 us; the launch traced here: 148 us
  starting transfers between devices  69 us (46%)
  waiting for transfers between devices  49.2 us (33%)
  Pallas kernels  23 us (15%)
  other arithmetic  4.42 us (3%)
  local copies, waits for them, and re-layouts  1.9 us (1%)
    ppermute x3, starting transfers between devices, over_z(): return lax.ppermute(value, 'hst', [(i, i ^ 2 * k) for i in range(64)])  23.4 us
    pallas_call x7, Pallas kernels, call(): pl.pallas_call(kernel, out_shape=out_shape, in_specs=in_specs, out_specs=...  23 us
    ppermute x1, waiting for transfers between devices, shards(): other = lax.ppermute(other, 'head', [(i, i ^ 1) for i in range(8)])  18.5 us
    ppermute x1, starting transfers between devices, shards(): other = lax.ppermute(other, 'head', [(i, i ^ 1) for i in range(8)])  15.6 us
    all_to_all x2, waiting for transfers between devices, over_y(): return lax.all_to_all(value, 'hst', 0, 0, axis_index_groups=groups)  12.6 us
    ppermute x2, starting transfers between devices, over_core(): return lax.ppermute(value, 'hst', [(i, i ^ 1) for i in range(64)])  11.7 us
    all_to_all x2, waiting for transfers between devices, over_x(): lax.all_to_all(value, 'head', 0, 0, axis_index_groups=[[0, 2, 4, 6], [1,...  10.9 us
    all_to_all x2, starting transfers between devices, over_y(): return lax.all_to_all(value, 'hst', 0, 0, axis_index_groups=groups)  8.56 us
  transfers between devices with their start and end apart: 13, of which 7 were waited for; matrix products, arithmetic and copies ran while one was open for 2% of the time, Pallas kernels for 8%

commit v1 on v0

v1 whole, which is shorter than its diff:
```python
import math

import jax
import jax.numpy as jnp
from jax import lax
from jax.experimental import pallas as pl
from jax.experimental.pallas import tpu as pltpu
from jax.sharding import PartitionSpec as P

HD = 128
PASS = 128
ANCHOR = 128
GROUPS = 4
ROWS = 256
HALF = ROWS // 2
QROWS = ROWS * GROUPS
HROWS = HALF * GROUPS
TILE = 512
SCALE = math.log2(math.e) / math.sqrt(HD)
LOW = -1e30
BF = jnp.bfloat16
F32 = jnp.float32
VM = pl.BlockSpec(memory_space=pltpu.VMEM)
SM = pl.BlockSpec(memory_space=pltpu.SMEM)
HBM = pl.BlockSpec(memory_space=pltpu.HBM)


def dot_nt(a, b):
    return lax.dot_general(a, b, (((1,), (1,)), ((), ())), preferred_element_type=F32)


def fetch(pairs, sems):
    copies = [pltpu.make_async_copy(a, b, sems.at[i]) for i, (a, b) in enumerate(pairs)]
    for copy in copies:
        copy.start()
    return copies


def wait(copies):
    for copy in copies:
        copy.wait()


def prepare(index_hbm, key_hbm, value_hbm, passed_ref, anchor_ref, index_ref, both_ref, sems):
    wait(
        fetch(
            [(index_hbm, index_ref), (key_hbm, both_ref.at[:, :HD]), (value_hbm, both_ref.at[:, HD:])],
            sems,
        )
    )
    rows = lax.broadcasted_iota(jnp.int32, (ROWS, PASS), 0)
    pick = jnp.where(rows == index_ref[...], 1.0, 0.0).astype(BF)
    both = both_ref[...]
    passed_ref[...] = lax.dot_general(
        pick, both, (((0,), (0,)), ((), ())), preferred_element_type=F32
    ).astype(BF)
    anchor_ref[...] = both[:ANCHOR]


def pack(*refs):
    *pieces, out_ref = refs
    start = 0
    for piece in pieces:
        size = piece.shape[0]
        if len(out_ref.shape) == 2:
            out_ref[start : start + size] = piece[...]
        else:
            for y in range(out_ref.shape[0]):
                out_ref[y, start : start + size] = piece[...]
        start += size


def position(place_ref):
    me = place_ref[0]
    return me // 16, lax.rem(me // 2, 8), lax.rem(me, 2)


def tile(heads_ref, acc_ref, top_ref, start, key, value, mask, first):
    span = slice(start, start + TILE)
    s = dot_nt(heads_ref[span], key)
    if mask is not None:
        s = jnp.where(mask, s, LOW)
    parts = [s[:, j * HD : (j + 1) * HD] for j in range(s.shape[1] // HD)]
    high = parts[0]
    for part in parts[1:]:
        high = jnp.maximum(high, part)
    high = jnp.max(high, axis=1, keepdims=True)
    if first:
        new = jnp.broadcast_to(high, (TILE, HD))
    else:
        old = top_ref[span]
        new = jnp.maximum(old, high)
    weights = jnp.concatenate([jnp.exp2((part - new) * SCALE).astype(BF) for part in parts], axis=1)
    total = jnp.dot(weights, value, preferred_element_type=F32)
    if not first:
        shrink = jnp.exp2((old - new) * SCALE)
        total = acc_ref[span] * jnp.concatenate([shrink, shrink], axis=1) + total
    acc_ref[span] = total
    top_ref[span] = new


def attend(heads_ref, acc_ref, top_ref, block, mask=None, first=False):
    key, count = block[:, :HD], block.shape[0]
    value = jnp.concatenate([block[:, HD:], jnp.ones((count, HD), BF)], axis=1)
    for number in range(QROWS // TILE):
        one = mask(number) if mask is not None else None
        tile(heads_ref, acc_ref, top_ref, number * TILE, key, value, one, first)


def own_tokens(query_ref, local_ref, heads_ref, acc_ref, top_ref):
    for half in range(2):
        for g in range(GROUPS):
            start = half * HROWS + g * HALF
            heads_ref[start : start + HALF, :] = query_ref[half * HALF : (half + 1) * HALF, g * HD : (g + 1) * HD]
    token = lax.broadcasted_iota(jnp.int32, (TILE, ROWS), 0) % HALF
    key = lax.broadcasted_iota(jnp.int32, (TILE, ROWS), 1)

    def causal(number):
        return key <= token + (number * TILE // HROWS) * HALF

    attend(heads_ref, acc_ref, top_ref, local_ref[...], causal, first=True)


NEAR = (0, 4, 2, 6)
FAR = (1, 5, 3, 7)


def visit(place_ref, heads_ref, acc_ref, top_ref, pieces_ref, spots):
    y, z, c = position(place_ref)
    count = len(spots) * PASS
    lane = lax.broadcasted_iota(jnp.int32, (1, count), 1) // PASS

    @pl.loop(0, y + 1)
    def _(row):
        for side in range(2):
            core = c if side == 0 else 1 - c
            seen = jnp.zeros((1, count), jnp.int32)
            for spot, k in enumerate(spots):
                before = lax.rem(z // (1 << (k.bit_length() - 1)), 2) == 1 if k else core < c
                seen = jnp.where(lane == spot, (before | (row < y)).astype(jnp.int32), seen)
            attend(heads_ref, acc_ref, top_ref, pieces_ref[side, row, :count], lambda number: seen > 0)


def visit_anchor(place_ref, heads_ref, acc_ref, top_ref, pieces_ref):
    me = place_ref[0]

    @pl.when(me > 0)
    def _():
        attend(heads_ref, acc_ref, top_ref, pieces_ref[lax.rem(me, 2), 0, 4 * PASS :])


def attend_own(
    place_ref, query_hbm, key_hbm, value_hbm, heads_hbm, acc_hbm, top_hbm,
    query_ref, local_ref, heads_ref, acc_ref, top_ref, sems,
):
    wait(
        fetch(
            [(query_hbm, query_ref), (key_hbm, local_ref.at[:, :HD]), (value_hbm, local_ref.at[:, HD:])],
            sems,
        )
    )
    own_tokens(query_ref, local_ref, heads_ref, acc_ref, top_ref)
    wait(fetch([(heads_ref, heads_hbm), (acc_ref, acc_hbm), (top_ref, top_hbm)], sems))


def attend_near(
    place_ref, heads_hbm, acc_hbm, top_hbm, two_hbm, two2_hbm, pair_hbm, pair2_hbm, acc_out, top_out,
    pieces_ref, heads_ref, acc_ref, top_ref, sems,
):
    wait(
        fetch(
            [
                (heads_hbm, heads_ref),
                (acc_hbm, acc_ref),
                (top_hbm, top_ref),
                (two_hbm, pieces_ref.at[0, :, : 2 * PASS]),
                (two2_hbm, pieces_ref.at[1, :, : 2 * PASS]),
                (pair_hbm, pieces_ref.at[0, :, 2 * PASS :]),
                (pair2_hbm, pieces_ref.at[1, :, 2 * PASS :]),
            ],
            sems,
        )
    )
    visit(place_ref, heads_ref, acc_ref, top_ref, pieces_ref, NEAR)
    wait(fetch([(acc_ref, acc_out), (top_ref, top_out)], sems))


def attend_far(
    place_ref, heads_hbm, acc_hbm, top_hbm, ours_hbm, theirs_hbm, weight_hbm, away_hbm, attended_hbm,
    out_ref, attended_ref, weight_ref, pieces_ref, heads_ref, acc_ref, top_ref, sems,
):
    copies = fetch(
        [
            (heads_hbm, heads_ref),
            (acc_hbm, acc_ref),
            (top_hbm, top_ref),
            (ours_hbm, pieces_ref.at[0]),
            (theirs_hbm, pieces_ref.at[1]),
        ],
        sems,
    )
    wait(copies)
    weights = fetch([(weight_hbm, weight_ref)], sems.at[5:])
    visit(place_ref, heads_ref, acc_ref, top_ref, pieces_ref, FAR)
    visit_anchor(place_ref, heads_ref, acc_ref, top_ref, pieces_ref)
    result = (acc_ref[:, :HD] / acc_ref[:, HD:]).astype(BF)
    attended = jnp.concatenate(
        [
            jnp.concatenate(
                [result[half * HROWS + g * HALF : half * HROWS + (g + 1) * HALF] for g in range(GROUPS)], axis=1
            )
            for half in range(2)
        ],
        axis=0,
    )
    attended_ref[...] = attended
    sent = [pltpu.make_async_copy(attended_ref, attended_hbm, sems.at[0])]
    sent[0].start()
    wait(weights)
    sent += project(attended, weight_ref, 1 - lax.rem(place_ref[1], 2), out_ref, away_hbm, sems.at[1:])
    wait(sent)


def project(rows, weight_ref, side, out_ref, out_hbm, sems):
    width = out_ref.shape[2]
    sent = []
    for x in range(4):
        columns = pl.ds(pl.multiple_of((2 * x + side) * width, width), width)
        out_ref[x] = jnp.dot(rows, weight_ref[:, columns], preferred_element_type=F32).astype(BF)
        sent += fetch([(out_ref.at[x], out_hbm.at[x])], sems.at[x : x + 1])
    return sent


def project_home(place_ref, rows_hbm, weight_hbm, home_hbm, out_ref, rows_ref, weight_ref, sems):
    wait(fetch([(rows_hbm, rows_ref), (weight_hbm, weight_ref)], sems))
    wait(project(rows_ref[...], weight_ref, lax.rem(place_ref[1], 2), out_ref, home_hbm, sems.at[2:]))


def widen(value_ref, out_ref):
    out_ref[...] = value_ref[...].astype(F32)


def add_up(other_ref, parts_ref, out_ref):
    total = other_ref[...]
    for x in range(4):
        total = total + parts_ref[x].astype(F32)
    out_ref[...] = total.astype(BF)


def shape(*dims, dtype=BF):
    return jax.ShapeDtypeStruct(dims, dtype)


def shards(queries, keys, values, passing_index, out_weight):
    me = lax.axis_index("hst")
    head = lax.axis_index("head")

    def over_z(value, k):
        return lax.ppermute(value, "hst", [(i, i ^ (2 * k)) for i in range(64)])

    def over_core(value):
        return lax.ppermute(value, "hst", [(i, i ^ 1) for i in range(64)])

    def over_y(value):
        groups = [[16 * row + i for row in range(4)] for i in range(16)]
        return lax.all_to_all(value, "hst", 0, 0, axis_index_groups=groups)

    place = jnp.stack([me, head]).astype(jnp.int32)

    def call(kernel, out_shape, in_specs, out_specs, *args, scratch=(), limit=int(63.75 * 2**20), flops=2**20):
        return pl.pallas_call(
            kernel,
            out_shape=out_shape,
            in_specs=in_specs,
            out_specs=out_specs,
            scratch_shapes=scratch,
            compiler_params=pltpu.CompilerParams(vmem_limit_bytes=limit),
            cost_estimate=pl.CostEstimate(flops=flops, bytes_accessed=2**16, transcendentals=0),
        )(*args)

    def spread(value, k):
        step = 2 * k
        sent = lax.ppermute(value, "hst", [(i, i + step) for i in range(0, 16, 2 * step)])
        return jnp.where((me < 16) & (me % (2 * step) == step), sent, value)

    def over_x(value):
        return lax.all_to_all(value, "head", 0, 0, axis_index_groups=[[0, 2, 4, 6], [1, 3, 5, 7]])

    copies = pltpu.SemaphoreType.DMA((7,))
    passed, anchor = call(
        prepare,
        (shape(PASS, 2 * HD), shape(ANCHOR, 2 * HD)),
        [HBM] * 3,
        (VM,) * 2,
        passing_index,
        keys,
        values,
        scratch=[pltpu.VMEM((1, PASS), jnp.int32), pltpu.VMEM((ROWS, 2 * HD), BF), copies],
    )

    def packed(*pieces, rows=(4,), flops=10**10):
        size = sum(piece.shape[0] for piece in pieces)
        return call(
            pack,
            shape(*rows, size, 2 * HD),
            [VM] * len(pieces),
            VM,
            *pieces,
            limit=8 * 2**20,
            flops=flops,
        )

    def joined(*pieces):
        return packed(*pieces, rows=(), flops=2**20)

    width = GROUPS * HD
    state = [
        pltpu.VMEM((QROWS, HD), BF),
        pltpu.VMEM((QROWS, 2 * HD), F32),
        pltpu.VMEM((QROWS, HD), F32),
        copies,
    ]
    sums = (shape(QROWS, 2 * HD, dtype=F32), shape(QROWS, HD, dtype=F32))
    mirror = over_z(passed, 4)
    anchor, queries = lax.optimization_barrier((spread(anchor, 4), queries))
    heads, acc, top = call(
        attend_own,
        (shape(QROWS, HD),) + sums,
        [SM] + [HBM] * 3,
        (HBM,) * 3,
        place,
        queries,
        keys,
        values,
        scratch=[pltpu.VMEM((ROWS, width), BF), pltpu.VMEM((ROWS, 2 * HD), BF)] + state,
        flops=10**10,
    )
    mirror, anchor, heads, acc, top = lax.optimization_barrier((mirror, anchor, heads, acc, top))
    two = joined(passed, mirror)
    two_b = packed(two)
    pair, anchor = lax.optimization_barrier((over_z(two, 2), spread(anchor, 2)))
    near = joined(two, pair)
    pair_b = packed(pair)
    far = packed(over_z(near, 1), spread(anchor, 1))
    two_y, pair_b = lax.optimization_barrier((over_y(two_b), pair_b))
    pair_y, far, two_y2 = lax.optimization_barrier((over_y(pair_b), far, over_core(two_y)))
    far_y = over_y(far)
    acc, top = call(
        attend_near,
        sums,
        [SM] + [HBM] * 7,
        (HBM,) * 2,
        place,
        heads,
        acc,
        top,
        two_y,
        two_y2,
        pair_y,
        over_core(pair_y),
        scratch=[pltpu.VMEM((2, 4, 4 * PASS, 2 * HD), BF)] + state,
    )
    far_y, acc, top = lax.optimization_barrier((far_y, acc, top))
    away, attended = call(
        attend_far,
        (shape(4, ROWS, width), shape(ROWS, width)),
        [SM] + [HBM] * 6,
        (HBM,) * 2,
        place,
        heads,
        acc,
        top,
        far_y,
        over_core(far_y),
        out_weight,
        scratch=[pltpu.VMEM((4, ROWS, width), BF), pltpu.VMEM((ROWS, width), BF), pltpu.VMEM(out_weight.shape, BF)]
        + [pltpu.VMEM((2,) + far_y.shape, BF)]
        + state,
    )

    home = call(
        project_home,
        shape(4, ROWS, width),
        [SM] + [HBM] * 2,
        HBM,
        place,
        attended,
        out_weight,
        scratch=[
            pltpu.VMEM((4, ROWS, width), BF),
            pltpu.VMEM((ROWS, width), BF),
            pltpu.VMEM(out_weight.shape, BF),
            copies,
        ],
        flops=10**10,
    )
    away, home = lax.optimization_barrier((over_x(away), home))
    other = jnp.sum(away.astype(F32), axis=0).astype(BF)
    other = lax.ppermute(other, "head", [(i, i ^ 1) for i in range(8)])
    parts = over_x(home)
    return call(
        add_up,
        shape(ROWS, width),
        [VM] * 2,
        VM,
        call(widen, shape(ROWS, width, dtype=F32), [VM], VM, other, limit=2**24, flops=10**11),
        parts,
        limit=2**24,
    )


def solution(mesh):
    in_specs = (
        P("hst", "head"),
        P("hst", "head"),
        P("hst", "head"),
        P("hst", None),
        P("head", None),
    )
    out_specs = P("hst", "head")
    return jax.shard_map(shards, mesh=mesh, in_specs=in_specs, out_specs=out_specs, check_vma=False)
```

time: 149 us -> 145 us (0.973)
  the two profiles are of different devices: /device:TPU:1 before, /device:TPU:473 now
where the time goes in v1:
time: 145 us; the launch traced here: 144 us
  starting transfers between devices  59.2 us (41%)
  waiting for transfers between devices  44.4 us (31%)
  Pallas kernels  36.2 us (25%)
  other arithmetic  2.96 us (2%)
    pallas_call x12, Pallas kernels, call(): pl.pallas_call(kernel, out_shape=out_shape, in_specs=in_specs, out_specs=...  36.2 us
    ppermute x1, waiting for transfers between devices, shards(): other = lax.ppermute(other, 'head', [(i, i ^ 1) for i in range(8)])  27.6 us
    ppermute x3, starting transfers between devices, over_core(): return lax.ppermute(value, 'hst', [(i, i ^ 1) for i in range(64)])  18.6 us
    ppermute x3, starting transfers between devices, over_z(): return lax.ppermute(value, 'hst', [(i, i ^ 2 * k) for i in range(64)])  14.3 us
    all_to_all x3, starting transfers between devices, over_y(): return lax.all_to_all(value, 'hst', 0, 0, axis_index_groups=groups)  12.5 us
    all_to_all x2, waiting for transfers between devices, over_x(): lax.all_to_all(value, 'head', 0, 0, axis_index_groups=[[0, 2, 4, 6], [1,...  10.4 us
    all_to_all x2, starting transfers between devices, over_x(): lax.all_to_all(value, 'head', 0, 0, axis_index_groups=[[0, 2, 4, 6], [1,...  7.78 us
    ppermute x3, waiting for transfers between devices, over_core(): return lax.ppermute(value, 'hst', [(i, i ^ 1) for i in range(64)])  4.98 us
  transfers between devices with their start and end apart: 15, of which 6 were waited for; matrix products, arithmetic and copies ran while one was open for 1% of the time, Pallas kernels for 15%

profile of v1, /device:TPU:473, one launch (start us, length us, event | category | flops | bytes accessed | tf_op | source)
XLA Modules:
  0.0 143.8 jit_solution(18107359461577204907)
XLA Ops:
  0.0 1.8 %shard_map.55 = (bf16[128,256]{1,0:T(8,128)(2,1)}, bf16[128,256]{1,0:T(8,128)(2,1)}) custom-call(s32[1,128]{1,0:T(1,128)} %index_hbm.1, bf16[256,128]{1,0:T(8,128)(2,1)} %key_hbm.3, bf16[256,128]{1,0:T(8,128)(2,1)} %value_hbm.3), custom_call_target="tpu_custom_call" | custom-call | flops 1048576 | bytes 65536 | tf_op jit(solution)/shard_map/pallas_call | solution.py:271
  1.8 5.2 %collective-permute-start = (bf16[128,256]{1,0:T(8,128)(2,1)}, bf16[128,256]{1,0:T(8,128)(2,1)S(1)}, u32[]{:S(2)}, u32[]{:S(2)}) collective-permute-start(bf16[128,256]{1,0:T(8,128)(2,1)} %get-tuple-element.33.refs_0_), channel_id=1, source_target_pairs={{0,64},{8,72},{16,80},{24,88},{32,96},{40,104},{48,112},{56,120},{... | collective-permute-start | bytes 196616 | tf_op jit(solution)/shard_map/ppermute | solution.py:259
  7.0 0.7 collective-permute-start.1
  7.7 0.6 pad_add_fusion.place_ref
  8.3 0.0 collective-permute-done.1
  8.3 0.8 broadcast_select_fusion.2
  9.2 0.0 copy-start
  9.2 3.6 %shard_map.56 = (bf16[1024,128]{1,0:T(8,128)(2,1)}, f32[1024,256]{1,0:T(8,128)}, f32[1024,128]{1,0:T(8,128)}) custom-call(s32[2]{0:T(128)} %pad_add_fusion.place_ref, bf16[256,512]{1,0:T(8,128)(2,1)} %query_hbm, bf16[256,128]{1,0:T(8,128)(2,1)} %key_hbm.3, bf16[256,128]{1,0:T(8,128)(2,1)} %value_hbm.3), custom_call_target="tpu_custom_call" | custom-call | flops 10000000000 | bytes 65536 | tf_op jit(solution)/shard_map/pallas_call | solution.py:271
  12.8 1.4 collective-permute-done.refs_1_
  14.2 0.0 copy-done
  14.2 0.7 collective-permute-start.3
  14.9 1.9 %collective-permute-start.2 = (bf16[256,256]{1,0:T(8,128)(2,1)S(1)}, bf16[256,256]{1,0:T(8,128)(2,1)S(1)}, u32[]{:S(2)}, u32[]{:S(2)}) collective-permute-start(bf16[256,256]{1,0:T(8,128)(2,1)S(1)} %shard_map.57.refs_0_), channel_id=1, source_target_pairs={{0,32},{8,40},{16,48},{24,56},{32,0},{40,8},{48,16},{56,24},{64,96... | collective-permute-start | bytes 393224 | tf_op jit(solution)/shard_map/ppermute | solution.py:259
  16.8 0.8 shard_map.58
  17.6 4.1 %all-to-all-start = ((bf16[4,256,256]{2,1,0:T(8,128)(2,1)}), bf16[4,256,256]{2,1,0:T(8,128)(2,1)S(1)}, u32[]{:S(2)}, u32[]{:S(2)}) async-start(bf16[4,256,256]{2,1,0:T(8,128)(2,1)} %shard_map.58), calls=%async_computation | async-start | bytes 1048576 | tf_op jit(solution)/shard_map/all_to_all | solution.py:266
  21.8 0.0 collective-permute-done.3
  21.8 0.0 collective-permute-done.2.refs_0_.refs_1_
  21.8 0.7 collective-permute-start.5
  22.5 7.2 %collective-permute-start.4 = (bf16[512,256]{1,0:T(8,128)(2,1)S(1)}, bf16[512,256]{1,0:T(8,128)(2,1)S(1)}, u32[]{:S(2)}, u32[]{:S(2)}) collective-permute-start(bf16[512,256]{1,0:T(8,128)(2,1)S(1)} %shard_map.60), channel_id=1, source_target_pairs={{0,16},{8,24},{16,0},{24,8},{32,48},{40,56},{48,32},{56,40},{64,80... | collective-permute-start | bytes 786440 | tf_op jit(solution)/shard_map/ppermute | solution.py:259
  29.7 0.8 shard_map.59
  30.5 0.0 collective-permute-done.5
  30.5 0.0 all-to-all-done.two_hbm
  30.6 0.0 copy-start.1
  30.6 4.1 %all-to-all-start.1 = ((bf16[4,256,256]{2,1,0:T(8,128)(2,1)}), bf16[4,256,256]{2,1,0:T(8,128)(2,1)S(1)}, u32[]{:S(2)}, u32[]{:S(2)}) async-start(bf16[4,256,256]{2,1,0:T(8,128)(2,1)} %shard_map.59), calls=%async_computation.1 | async-start | bytes 1048576 | tf_op jit(solution)/shard_map/all_to_all | solution.py:266
  34.7 9.7 %collective-permute-start.6 = (bf16[4,256,256]{2,1,0:T(8,128)(2,1)S(1)}, bf16[4,256,256]{2,1,0:T(8,128)(2,1)S(1)}, u32[]{:S(2)}, u32[]{:S(2)}) collective-permute-start(bf16[4,256,256]{2,1,0:T(8,128)(2,1)S(1)} %all-to-all-done.two_hbm), channel_id=1, source_target_pairs={{0,8},{8,0},{16,24},{24,16},{32,40},{40,32},{48,56},{56,48},{64,72... | collective-permute-start | bytes 1572872 | tf_op jit(solution)/shard_map/ppermute | solution.py:262
  44.4 0.0 collective-permute-done.4.refs_0_
  44.5 1.1 shard_map.61
  45.6 0.0 copy-done.1
  45.6 0.0 all-to-all-done.1.pair_hbm
  45.6 0.0 copy-start.2
  45.6 0.4 collective-permute-done.6.two2_hbm
  46.0 0.0 copy-start.3
  46.0 0.8 copy-done.3
  46.8 4.3 %all-to-all-start.2 = ((bf16[4,640,256]{2,1,0:T(8,128)(2,1)}), bf16[4,640,256]{2,1,0:T(8,128)(2,1)}, u32[]{:S(2)}, u32[]{:S(2)}) async-start(bf16[4,640,256]{2,1,0:T(8,128)(2,1)} %shard_map.61), calls=%async_computation.2 | async-start | bytes 2621440 | tf_op jit(solution)/shard_map/all_to_all | solution.py:266
  51.1 0.0 copy-done.2
  51.1 6.5 %collective-permute-start.7 = (bf16[4,256,256]{2,1,0:T(8,128)(2,1)S(1)}, bf16[4,256,256]{2,1,0:T(8,128)(2,1)}, u32[]{:S(2)}, u32[]{:S(2)}) collective-permute-start(bf16[4,256,256]{2,1,0:T(8,128)(2,1)S(1)} %all-to-all-done.1.pair_hbm), channel_id=1, source_target_pairs={{0,8},{8,0},{16,24},{24,16},{32,40},{40,32},{48,56},{56,48},{64,72... | collective-permute-start | bytes 1572872 | tf_op jit(solution)/shard_map/ppermute | solution.py:262
  57.6 1.6 %collective-permute-done.7.pair2_hbm = bf16[4,256,256]{2,1,0:T(8,128)(2,1)} collective-permute-done((bf16[4,256,256]{2,1,0:T(8,128)(2,1)S(1)}, bf16[4,256,256]{2,1,0:T(8,128)(2,1)}, u32[]{:S(2)}, u32[]{:S(2)}) %collective-permute-start.7) | collective-permute-done | bytes 524320 | tf_op jit(solution)/shard_map/ppermute | solution.py:262
  59.3 10.7 %shard_map.62 = (f32[1024,256]{1,0:T(8,128)}, f32[1024,128]{1,0:T(8,128)}) custom-call(s32[2]{0:T(128)} %pad_add_fusion.place_ref, bf16[1024,128]{1,0:T(8,128)(2,1)} %get-tuple-element.40.heads_hbm, f32[1024,256]{1,0:T(8,128)} %get-tuple-element.48.acc_hbm, f32[1024,128]{1,0:T(8,128)} %get-tuple-element.49.top_hbm, bf16[4,256,256]{2,1,0:T(8,128)(2,1)} %copy-done.1, ...), custom_call_target="tpu_custom_call" | custom-call | flops 1048576 | bytes 65536 | tf_op jit(solution)/shard_map/pallas_call | solution.py:271
  70.0 0.0 all-to-all-done.2.ours_hbm
  70.0 2.3 %collective-permute-start.8 = (bf16[4,640,256]{2,1,0:T(8,128)(2,1)}, bf16[4,640,256]{2,1,0:T(8,128)(2,1)}, u32[]{:S(2)}, u32[]{:S(2)}) collective-permute-start(bf16[4,640,256]{2,1,0:T(8,128)(2,1)} %all-to-all-done.2.ours_hbm), channel_id=1, source_target_pairs={{0,8},{8,0},{16,24},{24,16},{32,40},{40,32},{48,56},{56,48},{64,72... | collective-permute-start | bytes 3932168 | tf_op jit(solution)/shard_map/ppermute | solution.py:262
  72.3 3.0 %collective-permute-done.8.theirs_hbm = bf16[4,640,256]{2,1,0:T(8,128)(2,1)} collective-permute-done((bf16[4,640,256]{2,1,0:T(8,128)(2,1)}, bf16[4,640,256]{2,1,0:T(8,128)(2,1)}, u32[]{:S(2)}, u32[]{:S(2)}) %collective-permute-start.8) | collective-permute-done | bytes 1310752 | tf_op jit(solution)/shard_map/ppermute | solution.py:262
  75.3 12.0 %shard_map.63 = (bf16[4,256,512]{2,1,0:T(8,128)(2,1)}, bf16[256,512]{1,0:T(8,128)(2,1)}) custom-call(s32[2]{0:T(128)} %pad_add_fusion.place_ref, bf16[1024,128]{1,0:T(8,128)(2,1)} %get-tuple-element.40.heads_hbm, f32[1024,256]{1,0:T(8,128)} %get-tuple-element.54.acc_hbm, f32[1024,128]{1,0:T(8,128)} %get-tuple-element.55.top_hbm, ...), custom_call_target="tpu_custom_call" | custom-call | flops 1048576 | bytes 65536 | tf_op jit(solution)/shard_map/pallas_call | solution.py:271
  87.3 4.3 %all-to-all-start.3 = ((bf16[4,256,512]{2,1,0:T(8,128)(2,1)}), bf16[4,256,512]{2,1,0:T(8,128)(2,1)}, u32[]{:S(2)}, u32[]{:S(2)}) async-start(bf16[4,256,512]{2,1,0:T(8,128)(2,1)} %get-tuple-element.57), calls=%async_computation.3 | async-start | bytes 2097152 | tf_op jit(solution)/shard_map/all_to_all | solution.py:287
  91.6 4.4 %shard_map.64 = bf16[4,256,512]{2,1,0:T(8,128)(2,1)} custom-call(s32[2]{0:T(128)} %pad_add_fusion.place_ref, bf16[256,512]{1,0:T(8,128)(2,1)} %get-tuple-element.58.rows_hbm, bf16[512,4096]{1,0:T(8,128)(2,1)} %weight_hbm.3), custom_call_target="tpu_custom_call" | custom-call | flops 10000000000 | bytes 65536 | tf_op jit(solution)/shard_map/pallas_call | solution.py:271
  96.0 10.4 %all-to-all-done.3 = bf16[4,256,512]{2,1,0:T(8,128)(2,1)} async-done(((bf16[4,256,512]{2,1,0:T(8,128)(2,1)}), bf16[4,256,512]{2,1,0:T(8,128)(2,1)}, u32[]{:S(2)}, u32[]{:S(2)}) %all-to-all-start.3) | async-done | bytes 1048608 | tf_op jit(solution)/shard_map/all_to_all | solution.py:287
  106.4 1.5 %reduce_sum.12 = bf16[256,512]{1,0:T(8,128)(2,1)S(1)} reduce(bf16[4,256,512]{2,1,0:T(8,128)(2,1)} %all-to-all-done.3, bf16[]{:T(256)} %constant.46.clone.1), dimensions={0}, to_apply=%region_0.1 | reduce | flops 393216 | bytes 1310722 | tf_op jit(solution)/shard_map/reduce_sum | solution.py:398
  107.8 4.0 %collective-permute-start.9 = (bf16[256,512]{1,0:T(8,128)(2,1)S(1)}, bf16[256,512]{1,0:T(8,128)(2,1)S(1)}, u32[]{:S(2)}, u32[]{:S(2)}) collective-permute-start(bf16[256,512]{1,0:T(8,128)(2,1)S(1)} %reduce_sum.12), channel_id=1, source_target_pairs={{0,1},{1,0},{2,3},{3,2},{4,5},{5,4},{6,7},{7,6},{8,9},{9,8},{10,11... | collective-permute-start | bytes 786440 | tf_op jit(solution)/shard_map/ppermute | solution.py:399
  111.9 3.5 %all-to-all-start.4 = ((bf16[4,256,512]{2,1,0:T(8,128)(2,1)}), bf16[4,256,512]{2,1,0:T(8,128)(2,1)S(1)}, u32[]{:S(2)}, u32[]{:S(2)}) async-start(bf16[4,256,512]{2,1,0:T(8,128)(2,1)} %shard_map.64), calls=%async_computation.4 | async-start | bytes 2097152 | tf_op jit(solution)/shard_map/all_to_all | solution.py:287
  115.4 27.6 %collective-permute-done.9.value_ref = bf16[256,512]{1,0:T(8,128)(2,1)S(1)} collective-permute-done((bf16[256,512]{1,0:T(8,128)(2,1)S(1)}, bf16[256,512]{1,0:T(8,128)(2,1)S(1)}, u32[]{:S(2)}, u32[]{:S(2)}) %collective-permute-start.9) | collective-permute-done | bytes 262176 | tf_op jit(solution)/shard_map/ppermute | solution.py:399
  143.0 0.0 all-to-all-done.4.parts_ref
  143.0 0.9 shard_map.66
  (5 shorter events, 0.1 us)
Async XLA Ops:
  1.8 12.4 %collective-permute-start = (bf16[128,256]{1,0:T(8,128)(2,1)}, bf16[128,256]{1,0:T(8,128)(2,1)S(1)}, u32[]{:S(2)}, u32[]{:S(2)}) collective-permute-start(bf16[128,256]{1,0:T(8,128)(2,1)} %get-tuple-element.33.refs_0_), channel_id=1, source_target_pairs={{0,64},{8,72},{16,80},{24,88},{32,96},{40,104},{48,112},{56,120},{... | collective-permute-start | bytes 196616 | tf_op jit(solution)/shard_map/ppermute | solution.py:259
  7.0 1.4 collective-permute-start.1
  9.2 5.0 %copy-start = (bf16[128,256]{1,0:T(8,128)(2,1)S(1)}, bf16[128,256]{1,0:T(8,128)(2,1)}, u32[]{:S(2)}) copy-start(bf16[128,256]{1,0:T(8,128)(2,1)} %get-tuple-element.33.refs_0_) | copy-start | bytes 196612
  14.2 7.5 %collective-permute-start.3 = (bf16[128,256]{1,0:T(8,128)(2,1)S(1)}, bf16[128,256]{1,0:T(8,128)(2,1)S(1)}, u32[]{:S(2)}, u32[]{:S(2)}) collective-permute-start(bf16[128,256]{1,0:T(8,128)(2,1)S(1)} %broadcast_select_fusion.2), channel_id=1, source_target_pairs={{0,32},{64,96},{1,33},{65,97},{2,34},{66,98},{3,35},{67,99},{4,36}... | collective-permute-start | bytes 196616 | tf_op jit(solution)/shard_map/ppermute | solution.py:283
  14.9 6.9 %collective-permute-start.2 = (bf16[256,256]{1,0:T(8,128)(2,1)S(1)}, bf16[256,256]{1,0:T(8,128)(2,1)S(1)}, u32[]{:S(2)}, u32[]{:S(2)}) collective-permute-start(bf16[256,256]{1,0:T(8,128)(2,1)S(1)} %shard_map.57.refs_0_), channel_id=1, source_target_pairs={{0,32},{8,40},{16,48},{24,56},{32,0},{40,8},{48,16},{56,24},{64,96... | collective-permute-start | bytes 393224 | tf_op jit(solution)/shard_map/ppermute | solution.py:259
  17.6 12.9 %all-to-all-start = ((bf16[4,256,256]{2,1,0:T(8,128)(2,1)}), bf16[4,256,256]{2,1,0:T(8,128)(2,1)S(1)}, u32[]{:S(2)}, u32[]{:S(2)}) async-start(bf16[4,256,256]{2,1,0:T(8,128)(2,1)} %shard_map.58), calls=%async_computation | async-start | bytes 1048576 | tf_op jit(solution)/shard_map/all_to_all | solution.py:266
  21.8 8.7 %collective-permute-start.5 = (bf16[128,256]{1,0:T(8,128)(2,1)S(1)}, bf16[128,256]{1,0:T(8,128)(2,1)S(1)}, u32[]{:S(2)}, u32[]{:S(2)}) collective-permute-start(bf16[128,256]{1,0:T(8,128)(2,1)S(1)} %broadcast_select_fusion.1), channel_id=1, source_target_pairs={{0,16},{32,48},{64,80},{96,112},{1,17},{33,49},{65,81},{97,113},{2... | collective-permute-start | bytes 196616 | tf_op jit(solution)/shard_map/ppermute | solution.py:283
  22.5 22.0 %collective-permute-start.4 = (bf16[512,256]{1,0:T(8,128)(2,1)S(1)}, bf16[512,256]{1,0:T(8,128)(2,1)S(1)}, u32[]{:S(2)}, u32[]{:S(2)}) collective-permute-start(bf16[512,256]{1,0:T(8,128)(2,1)S(1)} %shard_map.60), channel_id=1, source_target_pairs={{0,16},{8,24},{16,0},{24,8},{32,48},{40,56},{48,32},{56,40},{64,80... | collective-permute-start | bytes 786440 | tf_op jit(solution)/shard_map/ppermute | solution.py:259
  30.6 15.0 %copy-start.1 = (bf16[4,256,256]{2,1,0:T(8,128)(2,1)}, bf16[4,256,256]{2,1,0:T(8,128)(2,1)S(1)}, u32[]{:S(2)}) copy-start(bf16[4,256,256]{2,1,0:T(8,128)(2,1)S(1)} %all-to-all-done.two_hbm) | copy-start | bytes 1572868
  30.6 15.0 %all-to-all-start.1 = ((bf16[4,256,256]{2,1,0:T(8,128)(2,1)}), bf16[4,256,256]{2,1,0:T(8,128)(2,1)S(1)}, u32[]{:S(2)}, u32[]{:S(2)}) async-start(bf16[4,256,256]{2,1,0:T(8,128)(2,1)} %shard_map.59), calls=%async_computation.1 | async-start | bytes 1048576 | tf_op jit(solution)/shard_map/all_to_all | solution.py:266
  34.7 11.3 %collective-permute-start.6 = (bf16[4,256,256]{2,1,0:T(8,128)(2,1)S(1)}, bf16[4,256,256]{2,1,0:T(8,128)(2,1)S(1)}, u32[]{:S(2)}, u32[]{:S(2)}) collective-permute-start(bf16[4,256,256]{2,1,0:T(8,128)(2,1)S(1)} %all-to-all-done.two_hbm), channel_id=1, source_target_pairs={{0,8},{8,0},{16,24},{24,16},{32,40},{40,32},{48,56},{56,48},{64,72... | collective-permute-start | bytes 1572872 | tf_op jit(solution)/shard_map/ppermute | solution.py:262
  45.6 5.5 %copy-start.2 = (bf16[4,256,256]{2,1,0:T(8,128)(2,1)}, bf16[4,256,256]{2,1,0:T(8,128)(2,1)S(1)}, u32[]{:S(2)}) copy-start(bf16[4,256,256]{2,1,0:T(8,128)(2,1)S(1)} %all-to-all-done.1.pair_hbm) | copy-start | bytes 1572868
  46.0 0.8 copy-start.3
  46.8 23.2 %all-to-all-start.2 = ((bf16[4,640,256]{2,1,0:T(8,128)(2,1)}), bf16[4,640,256]{2,1,0:T(8,128)(2,1)}, u32[]{:S(2)}, u32[]{:S(2)}) async-start(bf16[4,640,256]{2,1,0:T(8,128)(2,1)} %shard_map.61), calls=%async_computation.2 | async-start | bytes 2621440 | tf_op jit(solution)/shard_map/all_to_all | solution.py:266
  51.1 8.2 %collective-permute-start.7 = (bf16[4,256,256]{2,1,0:T(8,128)(2,1)S(1)}, bf16[4,256,256]{2,1,0:T(8,128)(2,1)}, u32[]{:S(2)}, u32[]{:S(2)}) collective-permute-start(bf16[4,256,256]{2,1,0:T(8,128)(2,1)S(1)} %all-to-all-done.1.pair_hbm), channel_id=1, source_target_pairs={{0,8},{8,0},{16,24},{24,16},{32,40},{40,32},{48,56},{56,48},{64,72... | collective-permute-start | bytes 1572872 | tf_op jit(solution)/shard_map/ppermute | solution.py:262
  70.0 5.3 %collective-permute-start.8 = (bf16[4,640,256]{2,1,0:T(8,128)(2,1)}, bf16[4,640,256]{2,1,0:T(8,128)(2,1)}, u32[]{:S(2)}, u32[]{:S(2)}) collective-permute-start(bf16[4,640,256]{2,1,0:T(8,128)(2,1)} %all-to-all-done.2.ours_hbm), channel_id=1, source_target_pairs={{0,8},{8,0},{16,24},{24,16},{32,40},{40,32},{48,56},{56,48},{64,72... | collective-permute-start | bytes 3932168 | tf_op jit(solution)/shard_map/ppermute | solution.py:262
  87.3 19.1 %all-to-all-start.3 = ((bf16[4,256,512]{2,1,0:T(8,128)(2,1)}), bf16[4,256,512]{2,1,0:T(8,128)(2,1)}, u32[]{:S(2)}, u32[]{:S(2)}) async-start(bf16[4,256,512]{2,1,0:T(8,128)(2,1)} %get-tuple-element.57), calls=%async_computation.3 | async-start | bytes 2097152 | tf_op jit(solution)/shard_map/all_to_all | solution.py:287
  107.8 35.1 %collective-permute-start.9 = (bf16[256,512]{1,0:T(8,128)(2,1)S(1)}, bf16[256,512]{1,0:T(8,128)(2,1)S(1)}, u32[]{:S(2)}, u32[]{:S(2)}) collective-permute-start(bf16[256,512]{1,0:T(8,128)(2,1)S(1)} %reduce_sum.12), channel_id=1, source_target_pairs={{0,1},{1,0},{2,3},{3,2},{4,5},{5,4},{6,7},{7,6},{8,9},{9,8},{10,11... | collective-permute-start | bytes 786440 | tf_op jit(solution)/shard_map/ppermute | solution.py:399
  111.9 31.1 %all-to-all-start.4 = ((bf16[4,256,512]{2,1,0:T(8,128)(2,1)}), bf16[4,256,512]{2,1,0:T(8,128)(2,1)S(1)}, u32[]{:S(2)}, u32[]{:S(2)}) async-start(bf16[4,256,512]{2,1,0:T(8,128)(2,1)} %shard_map.64), calls=%async_computation.4 | async-start | bytes 2097152 | tf_op jit(solution)/shard_map/all_to_all | solution.py:287

commit v2 on v1

--- a/solution.py
+++ b/solution.py
@@ -236,6 +236,13 @@
     wait(project(rows_ref[...], weight_ref, lax.rem(place_ref[1], 2), out_ref, home_hbm, sems.at[2:]))
 
 
+def sum_parts(parts_ref, out_ref):
+    total = parts_ref[0].astype(F32)
+    for x in range(1, 4):
+        total = total + parts_ref[x].astype(F32)
+    out_ref[...] = total.astype(BF)
+
+
 def widen(value_ref, out_ref):
     out_ref[...] = value_ref[...].astype(F32)
 
@@ -287,6 +294,7 @@
         return lax.all_to_all(value, "head", 0, 0, axis_index_groups=[[0, 2, 4, 6], [1, 3, 5, 7]])
 
     copies = pltpu.SemaphoreType.DMA((7,))
+    three = pltpu.SemaphoreType.DMA((3,))
     passed, anchor = call(
         prepare,
         (shape(PASS, 2 * HD), shape(ANCHOR, 2 * HD)),
@@ -295,7 +303,7 @@
         passing_index,
         keys,
         values,
-        scratch=[pltpu.VMEM((1, PASS), jnp.int32), pltpu.VMEM((ROWS, 2 * HD), BF), copies],
+        scratch=[pltpu.VMEM((1, PASS), jnp.int32), pltpu.VMEM((ROWS, 2 * HD), BF), three],
     )
 
     def packed(*pieces, rows=(4,), flops=10**10):
@@ -358,6 +366,7 @@
         two_y2,
         pair_y,
         over_core(pair_y),
+        limit=3 * 2**23,
         scratch=[pltpu.VMEM((2, 4, 4 * PASS, 2 * HD), BF)] + state,
     )
     far_y, acc, top = lax.optimization_barrier((far_y, acc, top))
@@ -392,10 +401,11 @@
             pltpu.VMEM(out_weight.shape, BF),
             copies,
         ],
+        limit=2**24,
         flops=10**10,
     )
     away, home = lax.optimization_barrier((over_x(away), home))
-    other = jnp.sum(away.astype(F32), axis=0).astype(BF)
+    other = call(sum_parts, shape(ROWS, width), [VM], VM, away, limit=2**24)
     other = lax.ppermute(other, "head", [(i, i ^ 1) for i in range(8)])
     parts = over_x(home)
     return call(

time: 145 us -> 141 us (0.972)
  Pallas kernels: 36.2 us -> 31.3 us
  local copies, waits for them, and re-layouts: 0.82 us -> 3.98 us
  other arithmetic: 2.96 us -> 1.45 us
    pallas_call x12 -> x13, Pallas kernels: 36.2 us -> 31.3 us  [call(): pl.pallas_call(kernel, out_shape=out_shape, in_specs=in_specs, out_specs=...]
    unnamed x8 -> x20, local copies, waits for them, and re-layouts: 0.82 us -> 3.98 us
    reduce_sum x1 -> x0, other arithmetic: 1.45 us -> none  [shards(): other = jnp.sum(away.astype(F32), axis=0).astype(BF)]
  transfers between devices with their start and end apart: 15 -> 15, of which waited for: 6 -> 6; matrix products, arithmetic and copies ran while one was open for 1% -> 1% of each run, Pallas kernels for 15% -> 12%
where the time goes in v2:
time: 141 us; the launch traced here: 140 us
  starting transfers between devices  58.8 us (42%)
  waiting for transfers between devices  44.2 us (31%)
  Pallas kernels  31.3 us (22%)
  local copies, waits for them, and re-layouts  3.98 us (3%)
  other arithmetic  1.45 us (1%)
    pallas_call x13, Pallas kernels, call(): pl.pallas_call(kernel, out_shape=out_shape, in_specs=in_specs, out_specs=...  31.3 us
    ppermute x1, waiting for transfers between devices, shards(): other = lax.ppermute(other, 'head', [(i, i ^ 1) for i in range(8)])  27.9 us
    ppermute x3, starting transfers between devices, over_core(): return lax.ppermute(value, 'hst', [(i, i ^ 1) for i in range(64)])  18.4 us
    ppermute x3, starting transfers between devices, over_z(): return lax.ppermute(value, 'hst', [(i, i ^ 2 * k) for i in range(64)])  14.3 us
    all_to_all x3, starting transfers between devices, over_y(): return lax.all_to_all(value, 'hst', 0, 0, axis_index_groups=groups)  12.7 us
    all_to_all x2, waiting for transfers between devices, over_x(): lax.all_to_all(value, 'head', 0, 0, axis_index_groups=[[0, 2, 4, 6], [1,...  9.99 us
    all_to_all x2, starting transfers between devices, over_x(): lax.all_to_all(value, 'head', 0, 0, axis_index_groups=[[0, 2, 4, 6], [1,...  7.68 us
    ppermute x3, waiting for transfers between devices, over_core(): return lax.ppermute(value, 'hst', [(i, i ^ 1) for i in range(64)])  4.82 us
  transfers between devices with their start and end apart: 15, of which 6 were waited for; matrix products, arithmetic and copies ran while one was open for 1% of the time, Pallas kernels for 12%

profile of v2, /device:TPU:473, one launch (start us, length us, event | category | flops | bytes accessed | tf_op | source)
XLA Modules:
  0.0 140.0 jit_solution(10557182457630792154)
XLA Ops:
  0.0 1.7 %shard_map.55 = (bf16[128,256]{1,0:T(8,128)(2,1)}, bf16[128,256]{1,0:T(8,128)(2,1)}) custom-call(s32[1,128]{1,0:T(1,128)} %index_hbm.1, bf16[256,128]{1,0:T(8,128)(2,1)} %key_hbm.3, bf16[256,128]{1,0:T(8,128)(2,1)} %value_hbm.3), custom_call_target="tpu_custom_call" | custom-call | flops 1048576 | bytes 65536 | tf_op jit(solution)/shard_map/pallas_call | solution.py:278
  1.7 5.2 %collective-permute-start = (bf16[128,256]{1,0:T(8,128)(2,1)}, bf16[128,256]{1,0:T(8,128)(2,1)S(1)}, u32[]{:S(2)}, u32[]{:S(2)}) collective-permute-start(bf16[128,256]{1,0:T(8,128)(2,1)} %get-tuple-element.33.refs_0_), channel_id=1, source_target_pairs={{0,64},{8,72},{16,80},{24,88},{32,96},{40,104},{48,112},{56,120},{... | collective-permute-start | bytes 196616 | tf_op jit(solution)/shard_map/ppermute | solution.py:266
  6.9 0.7 collective-permute-start.1
  7.6 0.6 pad_add_fusion.place_ref
  8.2 0.0 collective-permute-done.1
  8.2 0.8 broadcast_select_fusion.2
  9.1 0.0 copy-start.6
  9.1 3.6 %shard_map.56 = (bf16[1024,128]{1,0:T(8,128)(2,1)}, f32[1024,256]{1,0:T(8,128)}, f32[1024,128]{1,0:T(8,128)}) custom-call(s32[2]{0:T(128)} %pad_add_fusion.place_ref, bf16[256,512]{1,0:T(8,128)(2,1)} %query_hbm, bf16[256,128]{1,0:T(8,128)(2,1)} %key_hbm.3, bf16[256,128]{1,0:T(8,128)(2,1)} %value_hbm.3), custom_call_target="tpu_custom_call" | custom-call | flops 10000000000 | bytes 65536 | tf_op jit(solution)/shard_map/pallas_call | solution.py:278
  12.7 1.5 %collective-permute-done.refs_1_ = bf16[128,256]{1,0:T(8,128)(2,1)S(1)} collective-permute-done((bf16[128,256]{1,0:T(8,128)(2,1)}, bf16[128,256]{1,0:T(8,128)(2,1)S(1)}, u32[]{:S(2)}, u32[]{:S(2)}) %collective-permute-start) | collective-permute-done | bytes 65568 | tf_op jit(solution)/shard_map/ppermute | solution.py:266
  14.2 0.0 copy-done.6
  14.2 0.7 collective-permute-start.3
  14.9 1.9 %collective-permute-start.2 = (bf16[256,256]{1,0:T(8,128)(2,1)S(1)}, bf16[256,256]{1,0:T(8,128)(2,1)S(1)}, u32[]{:S(2)}, u32[]{:S(2)}) collective-permute-start(bf16[256,256]{1,0:T(8,128)(2,1)S(1)} %shard_map.57.refs_0_), channel_id=1, source_target_pairs={{0,32},{8,40},{16,48},{24,56},{32,0},{40,8},{48,16},{56,24},{64,96... | collective-permute-start | bytes 393224 | tf_op jit(solution)/shard_map/ppermute | solution.py:266
  16.8 0.8 shard_map.58
  17.6 4.1 %all-to-all-start = ((bf16[4,256,256]{2,1,0:T(8,128)(2,1)}), bf16[4,256,256]{2,1,0:T(8,128)(2,1)S(1)}, u32[]{:S(2)}, u32[]{:S(2)}) async-start(bf16[4,256,256]{2,1,0:T(8,128)(2,1)} %shard_map.58), calls=%async_computation | async-start | bytes 1048576 | tf_op jit(solution)/shard_map/all_to_all | solution.py:273
  21.8 0.0 collective-permute-done.3
  21.8 0.0 collective-permute-done.2.refs_0_.refs_1_
  21.8 0.7 collective-permute-start.5
  22.5 7.2 %collective-permute-start.4 = (bf16[512,256]{1,0:T(8,128)(2,1)S(1)}, bf16[512,256]{1,0:T(8,128)(2,1)S(1)}, u32[]{:S(2)}, u32[]{:S(2)}) collective-permute-start(bf16[512,256]{1,0:T(8,128)(2,1)S(1)} %shard_map.60), channel_id=1, source_target_pairs={{0,16},{8,24},{16,0},{24,8},{32,48},{40,56},{48,32},{56,40},{64,80... | collective-permute-start | bytes 786440 | tf_op jit(solution)/shard_map/ppermute | solution.py:266
  29.7 0.8 shard_map.59
  30.5 0.0 collective-permute-done.5
  30.5 0.0 all-to-all-done.two_hbm
  30.5 4.1 %all-to-all-start.1 = ((bf16[4,256,256]{2,1,0:T(8,128)(2,1)}), bf16[4,256,256]{2,1,0:T(8,128)(2,1)S(1)}, u32[]{:S(2)}, u32[]{:S(2)}) async-start(bf16[4,256,256]{2,1,0:T(8,128)(2,1)} %shard_map.59), calls=%async_computation.1 | async-start | bytes 1048576 | tf_op jit(solution)/shard_map/all_to_all | solution.py:273
  34.7 9.8 %collective-permute-start.6 = (bf16[4,256,256]{2,1,0:T(8,128)(2,1)S(1)}, bf16[4,256,256]{2,1,0:T(8,128)(2,1)S(1)}, u32[]{:S(2)}, u32[]{:S(2)}) collective-permute-start(bf16[4,256,256]{2,1,0:T(8,128)(2,1)S(1)} %all-to-all-done.two_hbm), channel_id=1, source_target_pairs={{0,8},{8,0},{16,24},{24,16},{32,40},{40,32},{48,56},{56,48},{64,72... | collective-permute-start | bytes 1572872 | tf_op jit(solution)/shard_map/ppermute | solution.py:269
  44.4 0.0 collective-permute-done.4.refs_0_
  44.4 1.2 shard_map.61
  45.6 0.0 copy-start.2
  45.6 0.0 copy-start.3
  45.6 0.0 copy-start.4
  45.6 0.0 copy-start.7
  45.6 0.0 all-to-all-done.1.pair_hbm
  45.6 0.3 collective-permute-done.6.two2_hbm
  45.9 4.4 %all-to-all-start.2 = ((bf16[4,640,256]{2,1,0:T(8,128)(2,1)}), bf16[4,640,256]{2,1,0:T(8,128)(2,1)}, u32[]{:S(2)}, u32[]{:S(2)}) async-start(bf16[4,640,256]{2,1,0:T(8,128)(2,1)} %shard_map.61), calls=%async_computation.2 | async-start | bytes 2621440 | tf_op jit(solution)/shard_map/all_to_all | solution.py:273
  50.4 6.4 %collective-permute-start.7 = (bf16[4,256,256]{2,1,0:T(8,128)(2,1)S(1)}, bf16[4,256,256]{2,1,0:T(8,128)(2,1)S(1)}, u32[]{:S(2)}, u32[]{:S(2)}) collective-permute-start(bf16[4,256,256]{2,1,0:T(8,128)(2,1)S(1)} %all-to-all-done.1.pair_hbm), channel_id=1, source_target_pairs={{0,8},{8,0},{16,24},{24,16},{32,40},{40,32},{48,56},{56,48},{64,72... | collective-permute-start | bytes 1572872 | tf_op jit(solution)/shard_map/ppermute | solution.py:269
  56.8 1.5 %collective-permute-done.7.pair2_hbm = bf16[4,256,256]{2,1,0:T(8,128)(2,1)S(1)} collective-permute-done((bf16[4,256,256]{2,1,0:T(8,128)(2,1)S(1)}, bf16[4,256,256]{2,1,0:T(8,128)(2,1)S(1)}, u32[]{:S(2)}, u32[]{:S(2)}) %collective-permute-start.7) | collective-permute-done | bytes 524320 | tf_op jit(solution)/shard_map/ppermute | solution.py:269
  58.3 0.0 copy-done.2
  58.3 0.0 copy-done.3
  58.3 0.0 copy-done.4
  58.3 0.0 copy-done.7
  58.3 7.8 %shard_map.62 = (f32[1024,256]{1,0:T(8,128)S(1)}, f32[1024,128]{1,0:T(8,128)S(1)}) custom-call(s32[2]{0:T(128)S(1)} %copy-done.7, bf16[1024,128]{1,0:T(8,128)(2,1)S(1)} %copy-done.2, f32[1024,256]{1,0:T(8,128)S(1)} %copy-done.3, f32[1024,128]{1,0:T(8,128)S(1)} %copy-done.4, bf16[4,256,256]{2,1,0:T(8,128)(2,1)S(1)} %all-to-all-done.two_hbm, ...), custom_call_target="tpu_custom_call" | custom-call | flops 1048576 | bytes 65536 | tf_op jit(solution)/shard_map/pallas_call | solution.py:278
  66.1 0.0 copy-start.1
  66.1 1.0 copy-done.1
  67.0 0.0 copy-start.5
  67.0 0.8 copy-done.5
  67.8 0.0 all-to-all-done.2.ours_hbm
  67.8 2.3 %collective-permute-start.8 = (bf16[4,640,256]{2,1,0:T(8,128)(2,1)}, bf16[4,640,256]{2,1,0:T(8,128)(2,1)}, u32[]{:S(2)}, u32[]{:S(2)}) collective-permute-start(bf16[4,640,256]{2,1,0:T(8,128)(2,1)} %all-to-all-done.2.ours_hbm), channel_id=1, source_target_pairs={{0,8},{8,0},{16,24},{24,16},{32,40},{40,32},{48,56},{56,48},{64,72... | collective-permute-start | bytes 3932168 | tf_op jit(solution)/shard_map/ppermute | solution.py:269
  70.1 3.0 %collective-permute-done.8.theirs_hbm = bf16[4,640,256]{2,1,0:T(8,128)(2,1)} collective-permute-done((bf16[4,640,256]{2,1,0:T(8,128)(2,1)}, bf16[4,640,256]{2,1,0:T(8,128)(2,1)}, u32[]{:S(2)}, u32[]{:S(2)}) %collective-permute-start.8) | collective-permute-done | bytes 1310752 | tf_op jit(solution)/shard_map/ppermute | solution.py:269
  73.1 12.0 %shard_map.63 = (bf16[4,256,512]{2,1,0:T(8,128)(2,1)}, bf16[256,512]{1,0:T(8,128)(2,1)}) custom-call(s32[2]{0:T(128)} %pad_add_fusion.place_ref, bf16[1024,128]{1,0:T(8,128)(2,1)} %get-tuple-element.40.heads_hbm, f32[1024,256]{1,0:T(8,128)} %copy-done.1, f32[1024,128]{1,0:T(8,128)} %copy-done.5, bf16[4,640,256]{2,1,0:T(8,128)(2,1)} %all-to-all-done.2.ours_hbm, ...), custom_call_target="tpu_custom_call" | custom-call | flops 1048576 | bytes 65536 | tf_op jit(solution)/shard_map/pallas_call | solution.py:278
  85.1 0.0 copy-start.8
  85.1 0.0 copy-start.9
  85.2 4.2 %all-to-all-start.3 = ((bf16[4,256,512]{2,1,0:T(8,128)(2,1)}), bf16[4,256,512]{2,1,0:T(8,128)(2,1)S(1)}, u32[]{:S(2)}, u32[]{:S(2)}) async-start(bf16[4,256,512]{2,1,0:T(8,128)(2,1)} %get-tuple-element.57), calls=%async_computation.3 | async-start | bytes 2097152 | tf_op jit(solution)/shard_map/all_to_all | solution.py:294
  89.3 0.0 copy-done.8
  89.3 0.0 copy-done.9
  89.3 0.0 copy-start
  89.3 2.2 %copy-done = bf16[512,4096]{1,0:T(8,128)(2,1)S(1)} copy-done((bf16[512,4096]{1,0:T(8,128)(2,1)S(1)}, bf16[512,4096]{1,0:T(8,128)(2,1)}, u32[]{:S(2)}) %copy-start) | copy-done | bytes 4194328
  91.5 2.3 %shard_map.64 = bf16[4,256,512]{2,1,0:T(8,128)(2,1)} custom-call(s32[2]{0:T(128)S(1)} %copy-done.8, bf16[256,512]{1,0:T(8,128)(2,1)S(1)} %copy-done.9, bf16[512,4096]{1,0:T(8,128)(2,1)S(1)} %copy-done), custom_call_target="tpu_custom_call" | custom-call | flops 10000000000 | bytes 65536 | tf_op jit(solution)/shard_map/pallas_call | solution.py:278
  93.9 10.0 %all-to-all-done.3.parts_ref = bf16[4,256,512]{2,1,0:T(8,128)(2,1)S(1)} async-done(((bf16[4,256,512]{2,1,0:T(8,128)(2,1)}), bf16[4,256,512]{2,1,0:T(8,128)(2,1)S(1)}, u32[]{:S(2)}, u32[]{:S(2)}) %all-to-all-start.3) | async-done | bytes 1048608 | tf_op jit(solution)/shard_map/all_to_all | solution.py:294
  103.8 0.1 shard_map.65
  104.0 3.7 %collective-permute-start.9 = (bf16[256,512]{1,0:T(8,128)(2,1)S(1)}, bf16[256,512]{1,0:T(8,128)(2,1)S(1)}, u32[]{:S(2)}, u32[]{:S(2)}) collective-permute-start(bf16[256,512]{1,0:T(8,128)(2,1)S(1)} %shard_map.65), channel_id=1, source_target_pairs={{0,1},{1,0},{2,3},{3,2},{4,5},{5,4},{6,7},{7,6},{8,9},{9,8},{10,11... | collective-permute-start | bytes 786440 | tf_op jit(solution)/shard_map/ppermute | solution.py:409
  107.7 3.5 %all-to-all-start.4 = ((bf16[4,256,512]{2,1,0:T(8,128)(2,1)}), bf16[4,256,512]{2,1,0:T(8,128)(2,1)S(1)}, u32[]{:S(2)}, u32[]{:S(2)}) async-start(bf16[4,256,512]{2,1,0:T(8,128)(2,1)} %shard_map.64), calls=%async_computation.4 | async-start | bytes 2097152 | tf_op jit(solution)/shard_map/all_to_all | solution.py:294
  111.2 27.9 %collective-permute-done.9.value_ref = bf16[256,512]{1,0:T(8,128)(2,1)S(1)} collective-permute-done((bf16[256,512]{1,0:T(8,128)(2,1)S(1)}, bf16[256,512]{1,0:T(8,128)(2,1)S(1)}, u32[]{:S(2)}, u32[]{:S(2)}) %collective-permute-start.9) | collective-permute-done | bytes 262176 | tf_op jit(solution)/shard_map/ppermute | solution.py:409
  139.2 0.0 all-to-all-done.4.parts_ref
  139.2 0.9 shard_map.67
  (5 shorter events, 0.1 us)
Async XLA Ops:
  1.7 12.4 %collective-permute-start = (bf16[128,256]{1,0:T(8,128)(2,1)}, bf16[128,256]{1,0:T(8,128)(2,1)S(1)}, u32[]{:S(2)}, u32[]{:S(2)}) collective-permute-start(bf16[128,256]{1,0:T(8,128)(2,1)} %get-tuple-element.33.refs_0_), channel_id=1, source_target_pairs={{0,64},{8,72},{16,80},{24,88},{32,96},{40,104},{48,112},{56,120},{... | collective-permute-start | bytes 196616 | tf_op jit(solution)/shard_map/ppermute | solution.py:266
  6.9 1.3 collective-permute-start.1
  9.1 5.1 %copy-start.6 = (bf16[128,256]{1,0:T(8,128)(2,1)S(1)}, bf16[128,256]{1,0:T(8,128)(2,1)}, u32[]{:S(2)}) copy-start(bf16[128,256]{1,0:T(8,128)(2,1)} %get-tuple-element.33.refs_0_) | copy-start | bytes 196612
  14.2 7.6 %collective-permute-start.3 = (bf16[128,256]{1,0:T(8,128)(2,1)S(1)}, bf16[128,256]{1,0:T(8,128)(2,1)S(1)}, u32[]{:S(2)}, u32[]{:S(2)}) collective-permute-start(bf16[128,256]{1,0:T(8,128)(2,1)S(1)} %broadcast_select_fusion.2), channel_id=1, source_target_pairs={{0,32},{64,96},{1,33},{65,97},{2,34},{66,98},{3,35},{67,99},{4,36}... | collective-permute-start | bytes 196616 | tf_op jit(solution)/shard_map/ppermute | solution.py:290
  14.9 6.9 %collective-permute-start.2 = (bf16[256,256]{1,0:T(8,128)(2,1)S(1)}, bf16[256,256]{1,0:T(8,128)(2,1)S(1)}, u32[]{:S(2)}, u32[]{:S(2)}) collective-permute-start(bf16[256,256]{1,0:T(8,128)(2,1)S(1)} %shard_map.57.refs_0_), channel_id=1, source_target_pairs={{0,32},{8,40},{16,48},{24,56},{32,0},{40,8},{48,16},{56,24},{64,96... | collective-permute-start | bytes 393224 | tf_op jit(solution)/shard_map/ppermute | solution.py:266
  17.6 12.9 %all-to-all-start = ((bf16[4,256,256]{2,1,0:T(8,128)(2,1)}), bf16[4,256,256]{2,1,0:T(8,128)(2,1)S(1)}, u32[]{:S(2)}, u32[]{:S(2)}) async-start(bf16[4,256,256]{2,1,0:T(8,128)(2,1)} %shard_map.58), calls=%async_computation | async-start | bytes 1048576 | tf_op jit(solution)/shard_map/all_to_all | solution.py:273
  21.8 8.7 %collective-permute-start.5 = (bf16[128,256]{1,0:T(8,128)(2,1)S(1)}, bf16[128,256]{1,0:T(8,128)(2,1)S(1)}, u32[]{:S(2)}, u32[]{:S(2)}) collective-permute-start(bf16[128,256]{1,0:T(8,128)(2,1)S(1)} %broadcast_select_fusion.1), channel_id=1, source_target_pairs={{0,16},{32,48},{64,80},{96,112},{1,17},{33,49},{65,81},{97,113},{2... | collective-permute-start | bytes 196616 | tf_op jit(solution)/shard_map/ppermute | solution.py:290
  22.5 21.9 %collective-permute-start.4 = (bf16[512,256]{1,0:T(8,128)(2,1)S(1)}, bf16[512,256]{1,0:T(8,128)(2,1)S(1)}, u32[]{:S(2)}, u32[]{:S(2)}) collective-permute-start(bf16[512,256]{1,0:T(8,128)(2,1)S(1)} %shard_map.60), channel_id=1, source_target_pairs={{0,16},{8,24},{16,0},{24,8},{32,48},{40,56},{48,32},{56,40},{64,80... | collective-permute-start | bytes 786440 | tf_op jit(solution)/shard_map/ppermute | solution.py:266
  30.5 15.1 %all-to-all-start.1 = ((bf16[4,256,256]{2,1,0:T(8,128)(2,1)}), bf16[4,256,256]{2,1,0:T(8,128)(2,1)S(1)}, u32[]{:S(2)}, u32[]{:S(2)}) async-start(bf16[4,256,256]{2,1,0:T(8,128)(2,1)} %shard_map.59), calls=%async_computation.1 | async-start | bytes 1048576 | tf_op jit(solution)/shard_map/all_to_all | solution.py:273
  34.7 11.3 %collective-permute-start.6 = (bf16[4,256,256]{2,1,0:T(8,128)(2,1)S(1)}, bf16[4,256,256]{2,1,0:T(8,128)(2,1)S(1)}, u32[]{:S(2)}, u32[]{:S(2)}) collective-permute-start(bf16[4,256,256]{2,1,0:T(8,128)(2,1)S(1)} %all-to-all-done.two_hbm), channel_id=1, source_target_pairs={{0,8},{8,0},{16,24},{24,16},{32,40},{40,32},{48,56},{56,48},{64,72... | collective-permute-start | bytes 1572872 | tf_op jit(solution)/shard_map/ppermute | solution.py:269
  45.6 12.7 %copy-start.2 = (bf16[1024,128]{1,0:T(8,128)(2,1)S(1)}, bf16[1024,128]{1,0:T(8,128)(2,1)}, u32[]{:S(2)}) copy-start(bf16[1024,128]{1,0:T(8,128)(2,1)} %get-tuple-element.40.heads_hbm) | copy-start | bytes 786436
  45.6 12.7 %copy-start.3 = (f32[1024,256]{1,0:T(8,128)S(1)}, f32[1024,256]{1,0:T(8,128)}, u32[]{:S(2)}) copy-start(f32[1024,256]{1,0:T(8,128)} %get-tuple-element.48.acc_hbm) | copy-start | bytes 3145732
  45.6 12.7 %copy-start.4 = (f32[1024,128]{1,0:T(8,128)S(1)}, f32[1024,128]{1,0:T(8,128)}, u32[]{:S(2)}) copy-start(f32[1024,128]{1,0:T(8,128)} %get-tuple-element.49.top_hbm) | copy-start | bytes 1572868
  45.6 12.7 %copy-start.7 = (s32[2]{0:T(128)S(1)}, s32[2]{0:T(128)}, u32[]{:S(2)}) copy-start(s32[2]{0:T(128)} %pad_add_fusion.place_ref) | copy-start | bytes 28
  45.9 21.9 %all-to-all-start.2 = ((bf16[4,640,256]{2,1,0:T(8,128)(2,1)}), bf16[4,640,256]{2,1,0:T(8,128)(2,1)}, u32[]{:S(2)}, u32[]{:S(2)}) async-start(bf16[4,640,256]{2,1,0:T(8,128)(2,1)} %shard_map.61), calls=%async_computation.2 | async-start | bytes 2621440 | tf_op jit(solution)/shard_map/all_to_all | solution.py:273
  50.4 7.9 %collective-permute-start.7 = (bf16[4,256,256]{2,1,0:T(8,128)(2,1)S(1)}, bf16[4,256,256]{2,1,0:T(8,128)(2,1)S(1)}, u32[]{:S(2)}, u32[]{:S(2)}) collective-permute-start(bf16[4,256,256]{2,1,0:T(8,128)(2,1)S(1)} %all-to-all-done.1.pair_hbm), channel_id=1, source_target_pairs={{0,8},{8,0},{16,24},{24,16},{32,40},{40,32},{48,56},{56,48},{64,72... | collective-permute-start | bytes 1572872 | tf_op jit(solution)/shard_map/ppermute | solution.py:269
  66.1 1.0 copy-start.1
  67.0 0.8 copy-start.5
  67.8 5.3 %collective-permute-start.8 = (bf16[4,640,256]{2,1,0:T(8,128)(2,1)}, bf16[4,640,256]{2,1,0:T(8,128)(2,1)}, u32[]{:S(2)}, u32[]{:S(2)}) collective-permute-start(bf16[4,640,256]{2,1,0:T(8,128)(2,1)} %all-to-all-done.2.ours_hbm), channel_id=1, source_target_pairs={{0,8},{8,0},{16,24},{24,16},{32,40},{40,32},{48,56},{56,48},{64,72... | collective-permute-start | bytes 3932168 | tf_op jit(solution)/shard_map/ppermute | solution.py:269
  85.1 4.2 %copy-start.8 = (s32[2]{0:T(128)S(1)}, s32[2]{0:T(128)}, u32[]{:S(2)}) copy-start(s32[2]{0:T(128)} %pad_add_fusion.place_ref) | copy-start | bytes 28
  85.1 4.2 %copy-start.9 = (bf16[256,512]{1,0:T(8,128)(2,1)S(1)}, bf16[256,512]{1,0:T(8,128)(2,1)}, u32[]{:S(2)}) copy-start(bf16[256,512]{1,0:T(8,128)(2,1)} %get-tuple-element.58.rows_hbm) | copy-start | bytes 786436
  85.2 18.7 %all-to-all-start.3 = ((bf16[4,256,512]{2,1,0:T(8,128)(2,1)}), bf16[4,256,512]{2,1,0:T(8,128)(2,1)S(1)}, u32[]{:S(2)}, u32[]{:S(2)}) async-start(bf16[4,256,512]{2,1,0:T(8,128)(2,1)} %get-tuple-element.57), calls=%async_computation.3 | async-start | bytes 2097152 | tf_op jit(solution)/shard_map/all_to_all | solution.py:294
  89.3 2.2 %copy-start = (bf16[512,4096]{1,0:T(8,128)(2,1)S(1)}, bf16[512,4096]{1,0:T(8,128)(2,1)}, u32[]{:S(2)}) copy-start(bf16[512,4096]{1,0:T(8,128)(2,1)} %weight_hbm.3) | copy-start | bytes 12582916
  104.0 35.1 %collective-permute-start.9 = (bf16[256,512]{1,0:T(8,128)(2,1)S(1)}, bf16[256,512]{1,0:T(8,128)(2,1)S(1)}, u32[]{:S(2)}, u32[]{:S(2)}) collective-permute-start(bf16[256,512]{1,0:T(8,128)(2,1)S(1)} %shard_map.65), channel_id=1, source_target_pairs={{0,1},{1,0},{2,3},{3,2},{4,5},{5,4},{6,7},{7,6},{8,9},{9,8},{10,11... | collective-permute-start | bytes 786440 | tf_op jit(solution)/shard_map/ppermute | solution.py:409
  107.7 31.4 %all-to-all-start.4 = ((bf16[4,256,512]{2,1,0:T(8,128)(2,1)}), bf16[4,256,512]{2,1,0:T(8,128)(2,1)S(1)}, u32[]{:S(2)}, u32[]{:S(2)}) async-start(bf16[4,256,512]{2,1,0:T(8,128)(2,1)} %shard_map.64), calls=%async_computation.4 | async-start | bytes 2097152 | tf_op jit(solution)/shard_map/all_to_all | solution.py:294

commit v3 on v2

--- a/solution.py
+++ b/solution.py
@@ -125,7 +125,7 @@
 FAR = (1, 5, 3, 7)
 
 
-def visit(place_ref, heads_ref, acc_ref, top_ref, pieces_ref, spots):
+def visit(place_ref, heads_ref, acc_ref, top_ref, piece, spots):
     y, z, c = position(place_ref)
     count = len(spots) * PASS
     lane = lax.broadcasted_iota(jnp.int32, (1, count), 1) // PASS
@@ -138,7 +138,7 @@
             for spot, k in enumerate(spots):
                 before = lax.rem(z // (1 << (k.bit_length() - 1)), 2) == 1 if k else core < c
                 seen = jnp.where(lane == spot, (before | (row < y)).astype(jnp.int32), seen)
-            attend(heads_ref, acc_ref, top_ref, pieces_ref[side, row, :count], lambda number: seen > 0)
+            attend(heads_ref, acc_ref, top_ref, piece(side, row), lambda number: seen > 0)
 
 
 def visit_anchor(place_ref, heads_ref, acc_ref, top_ref, pieces_ref):
@@ -164,25 +164,16 @@
 
 
 def attend_near(
-    place_ref, heads_hbm, acc_hbm, top_hbm, two_hbm, two2_hbm, pair_hbm, pair2_hbm, acc_out, top_out,
-    pieces_ref, heads_ref, acc_ref, top_ref, sems,
+    place_ref, heads_ref, acc_in, top_in, two_ref, two2_ref, pair_ref, pair2_ref, acc_ref, top_ref,
 ):
-    wait(
-        fetch(
-            [
-                (heads_hbm, heads_ref),
-                (acc_hbm, acc_ref),
-                (top_hbm, top_ref),
-                (two_hbm, pieces_ref.at[0, :, : 2 * PASS]),
-                (two2_hbm, pieces_ref.at[1, :, : 2 * PASS]),
-                (pair_hbm, pieces_ref.at[0, :, 2 * PASS :]),
-                (pair2_hbm, pieces_ref.at[1, :, 2 * PASS :]),
-            ],
-            sems,
-        )
-    )
-    visit(place_ref, heads_ref, acc_ref, top_ref, pieces_ref, NEAR)
-    wait(fetch([(acc_ref, acc_out), (top_ref, top_out)], sems))
+    acc_ref[...] = acc_in[...]
+    top_ref[...] = top_in[...]
+    sides = ((two_ref, pair_ref), (two2_ref, pair2_ref))
+
+    def piece(side, row):
+        return jnp.concatenate([ref[row] for ref in sides[side]], axis=0)
+
+    visit(place_ref, heads_ref, acc_ref, top_ref, piece, NEAR)
 
 
 def attend_far(
@@ -201,7 +192,7 @@
     )
     wait(copies)
     weights = fetch([(weight_hbm, weight_ref)], sems.at[5:])
-    visit(place_ref, heads_ref, acc_ref, top_ref, pieces_ref, FAR)
+    visit(place_ref, heads_ref, acc_ref, top_ref, lambda side, row: pieces_ref[side, row, : 4 * PASS], FAR)
     visit_anchor(place_ref, heads_ref, acc_ref, top_ref, pieces_ref)
     result = (acc_ref[:, :HD] / acc_ref[:, HD:]).astype(BF)
     attended = jnp.concatenate(
@@ -356,8 +347,8 @@
     acc, top = call(
         attend_near,
         sums,
-        [SM] + [HBM] * 7,
-        (HBM,) * 2,
+        [SM] + [VM] * 7,
+        (VM,) * 2,
         place,
         heads,
         acc,
@@ -367,7 +358,6 @@
         pair_y,
         over_core(pair_y),
         limit=3 * 2**23,
-        scratch=[pltpu.VMEM((2, 4, 4 * PASS, 2 * HD), BF)] + state,
     )
     far_y, acc, top = lax.optimization_barrier((far_y, acc, top))
     away, attended = call(

time: 141 us -> 141 us (level)
  no operation moved by 1% of the time
where the time goes in v3:
time: 141 us; the launch traced here: 140 us
  starting transfers between devices  58.8 us (42%)
  waiting for transfers between devices  44.2 us (31%)
  Pallas kernels  30.9 us (22%)
  local copies, waits for them, and re-layouts  3.98 us (3%)
  other arithmetic  1.45 us (1%)
    pallas_call x13, Pallas kernels, call(): pl.pallas_call(kernel, out_shape=out_shape, in_specs=in_specs, out_specs=...  30.9 us
    ppermute x1, waiting for transfers between devices, shards(): other = lax.ppermute(other, 'head', [(i, i ^ 1) for i in range(8)])  27.9 us
    ppermute x3, starting transfers between devices, over_core(): return lax.ppermute(value, 'hst', [(i, i ^ 1) for i in range(64)])  18.4 us
    ppermute x3, starting transfers between devices, over_z(): return lax.ppermute(value, 'hst', [(i, i ^ 2 * k) for i in range(64)])  14.3 us
    all_to_all x3, starting transfers between devices, over_y(): return lax.all_to_all(value, 'hst', 0, 0, axis_index_groups=groups)  12.7 us
    all_to_all x2, waiting for transfers between devices, over_x(): lax.all_to_all(value, 'head', 0, 0, axis_index_groups=[[0, 2, 4, 6], [1,...  9.98 us
    all_to_all x2, starting transfers between devices, over_x(): lax.all_to_all(value, 'head', 0, 0, axis_index_groups=[[0, 2, 4, 6], [1,...  7.68 us
    ppermute x3, waiting for transfers between devices, over_core(): return lax.ppermute(value, 'hst', [(i, i ^ 1) for i in range(64)])  4.82 us
  transfers between devices with their start and end apart: 15, of which 6 were waited for; matrix products, arithmetic and copies ran while one was open for 1% of the time, Pallas kernels for 12%

profile of v3, /device:TPU:473, one launch (start us, length us, event | category | flops | bytes accessed | tf_op | source)
XLA Modules:
  0.0 139.6 jit_solution(1396869347829952988)
XLA Ops:
  0.0 1.7 %shard_map.55 = (bf16[128,256]{1,0:T(8,128)(2,1)}, bf16[128,256]{1,0:T(8,128)(2,1)}) custom-call(s32[1,128]{1,0:T(1,128)} %index_hbm.1, bf16[256,128]{1,0:T(8,128)(2,1)} %key_hbm.3, bf16[256,128]{1,0:T(8,128)(2,1)} %value_hbm.3), custom_call_target="tpu_custom_call" | custom-call | flops 1048576 | bytes 65536 | tf_op jit(solution)/shard_map/pallas_call | solution.py:269
  1.7 5.2 %collective-permute-start = (bf16[128,256]{1,0:T(8,128)(2,1)}, bf16[128,256]{1,0:T(8,128)(2,1)S(1)}, u32[]{:S(2)}, u32[]{:S(2)}) collective-permute-start(bf16[128,256]{1,0:T(8,128)(2,1)} %get-tuple-element.33.refs_0_), channel_id=1, source_target_pairs={{0,64},{8,72},{16,80},{24,88},{32,96},{40,104},{48,112},{56,120},{... | collective-permute-start | bytes 196616 | tf_op jit(solution)/shard_map/ppermute | solution.py:257
  6.9 0.7 collective-permute-start.1
  7.6 0.6 pad_add_fusion.place_ref
  8.2 0.0 collective-permute-done.1
  8.2 0.8 broadcast_select_fusion.2
  9.1 0.0 copy-start.6
  9.1 3.6 %shard_map.56 = (bf16[1024,128]{1,0:T(8,128)(2,1)}, f32[1024,256]{1,0:T(8,128)}, f32[1024,128]{1,0:T(8,128)}) custom-call(s32[2]{0:T(128)} %pad_add_fusion.place_ref, bf16[256,512]{1,0:T(8,128)(2,1)} %query_hbm, bf16[256,128]{1,0:T(8,128)(2,1)} %key_hbm.3, bf16[256,128]{1,0:T(8,128)(2,1)} %value_hbm.3), custom_call_target="tpu_custom_call" | custom-call | flops 10000000000 | bytes 65536 | tf_op jit(solution)/shard_map/pallas_call | solution.py:269
  12.7 1.5 %collective-permute-done.refs_1_ = bf16[128,256]{1,0:T(8,128)(2,1)S(1)} collective-permute-done((bf16[128,256]{1,0:T(8,128)(2,1)}, bf16[128,256]{1,0:T(8,128)(2,1)S(1)}, u32[]{:S(2)}, u32[]{:S(2)}) %collective-permute-start) | collective-permute-done | bytes 65568 | tf_op jit(solution)/shard_map/ppermute | solution.py:257
  14.2 0.0 copy-done.6
  14.2 0.7 collective-permute-start.3
  14.9 1.9 %collective-permute-start.2 = (bf16[256,256]{1,0:T(8,128)(2,1)S(1)}, bf16[256,256]{1,0:T(8,128)(2,1)S(1)}, u32[]{:S(2)}, u32[]{:S(2)}) collective-permute-start(bf16[256,256]{1,0:T(8,128)(2,1)S(1)} %shard_map.57.refs_0_), channel_id=1, source_target_pairs={{0,32},{8,40},{16,48},{24,56},{32,0},{40,8},{48,16},{56,24},{64,96... | collective-permute-start | bytes 393224 | tf_op jit(solution)/shard_map/ppermute | solution.py:257
  16.8 0.8 shard_map.58
  17.6 4.1 %all-to-all-start = ((bf16[4,256,256]{2,1,0:T(8,128)(2,1)}), bf16[4,256,256]{2,1,0:T(8,128)(2,1)S(1)}, u32[]{:S(2)}, u32[]{:S(2)}) async-start(bf16[4,256,256]{2,1,0:T(8,128)(2,1)} %shard_map.58), calls=%async_computation | async-start | bytes 1048576 | tf_op jit(solution)/shard_map/all_to_all | solution.py:264
  21.8 0.0 collective-permute-done.3
  21.8 0.0 collective-permute-done.2.refs_0_.refs_1_
  21.8 0.7 collective-permute-start.5
  22.5 7.2 %collective-permute-start.4 = (bf16[512,256]{1,0:T(8,128)(2,1)S(1)}, bf16[512,256]{1,0:T(8,128)(2,1)S(1)}, u32[]{:S(2)}, u32[]{:S(2)}) collective-permute-start(bf16[512,256]{1,0:T(8,128)(2,1)S(1)} %shard_map.60), channel_id=1, source_target_pairs={{0,16},{8,24},{16,0},{24,8},{32,48},{40,56},{48,32},{56,40},{64,80... | collective-permute-start | bytes 786440 | tf_op jit(solution)/shard_map/ppermute | solution.py:257
  29.7 0.8 shard_map.59
  30.5 0.0 collective-permute-done.5
  30.5 0.0 all-to-all-done.two_ref
  30.5 4.1 %all-to-all-start.1 = ((bf16[4,256,256]{2,1,0:T(8,128)(2,1)}), bf16[4,256,256]{2,1,0:T(8,128)(2,1)S(1)}, u32[]{:S(2)}, u32[]{:S(2)}) async-start(bf16[4,256,256]{2,1,0:T(8,128)(2,1)} %shard_map.59), calls=%async_computation.1 | async-start | bytes 1048576 | tf_op jit(solution)/shard_map/all_to_all | solution.py:264
  34.7 9.8 %collective-permute-start.6 = (bf16[4,256,256]{2,1,0:T(8,128)(2,1)S(1)}, bf16[4,256,256]{2,1,0:T(8,128)(2,1)S(1)}, u32[]{:S(2)}, u32[]{:S(2)}) collective-permute-start(bf16[4,256,256]{2,1,0:T(8,128)(2,1)S(1)} %all-to-all-done.two_ref), channel_id=1, source_target_pairs={{0,8},{8,0},{16,24},{24,16},{32,40},{40,32},{48,56},{56,48},{64,72... | collective-permute-start | bytes 1572872 | tf_op jit(solution)/shard_map/ppermute | solution.py:260
  44.4 0.0 collective-permute-done.4.refs_0_
  44.4 1.2 shard_map.61
  45.6 0.0 copy-start.2
  45.6 0.0 copy-start.3
  45.6 0.0 copy-start.4
  45.6 0.0 copy-start.7
  45.6 0.0 all-to-all-done.1.pair_ref
  45.6 0.3 collective-permute-done.6.two2_ref
  45.9 4.4 %all-to-all-start.2 = ((bf16[4,640,256]{2,1,0:T(8,128)(2,1)}), bf16[4,640,256]{2,1,0:T(8,128)(2,1)}, u32[]{:S(2)}, u32[]{:S(2)}) async-start(bf16[4,640,256]{2,1,0:T(8,128)(2,1)} %shard_map.61), calls=%async_computation.2 | async-start | bytes 2621440 | tf_op jit(solution)/shard_map/all_to_all | solution.py:264
  50.4 6.4 %collective-permute-start.7 = (bf16[4,256,256]{2,1,0:T(8,128)(2,1)S(1)}, bf16[4,256,256]{2,1,0:T(8,128)(2,1)S(1)}, u32[]{:S(2)}, u32[]{:S(2)}) collective-permute-start(bf16[4,256,256]{2,1,0:T(8,128)(2,1)S(1)} %all-to-all-done.1.pair_ref), channel_id=1, source_target_pairs={{0,8},{8,0},{16,24},{24,16},{32,40},{40,32},{48,56},{56,48},{64,72... | collective-permute-start | bytes 1572872 | tf_op jit(solution)/shard_map/ppermute | solution.py:260
  56.8 1.5 %collective-permute-done.7.pair2_ref = bf16[4,256,256]{2,1,0:T(8,128)(2,1)S(1)} collective-permute-done((bf16[4,256,256]{2,1,0:T(8,128)(2,1)S(1)}, bf16[4,256,256]{2,1,0:T(8,128)(2,1)S(1)}, u32[]{:S(2)}, u32[]{:S(2)}) %collective-permute-start.7) | collective-permute-done | bytes 524320 | tf_op jit(solution)/shard_map/ppermute | solution.py:260
  58.3 0.0 copy-done.2
  58.3 0.0 copy-done.3
  58.3 0.0 copy-done.4
  58.3 0.0 copy-done.7
  58.3 7.4 %shard_map.62 = (f32[1024,256]{1,0:T(8,128)S(1)}, f32[1024,128]{1,0:T(8,128)S(1)}) custom-call(s32[2]{0:T(128)S(1)} %copy-done.7, bf16[1024,128]{1,0:T(8,128)(2,1)S(1)} %copy-done.2, f32[1024,256]{1,0:T(8,128)S(1)} %copy-done.3, f32[1024,128]{1,0:T(8,128)S(1)} %copy-done.4, bf16[4,256,256]{2,1,0:T(8,128)(2,1)S(1)} %all-to-all-done.two_ref, ...), custom_call_target="tpu_custom_call" | custom-call | flops 1048576 | bytes 65536 | tf_op jit(solution)/shard_map/pallas_call | solution.py:269
  65.7 0.0 copy-start.1
  65.7 1.0 copy-done.1
  66.6 0.0 copy-start.5
  66.6 0.8 copy-done.5
  67.4 0.0 all-to-all-done.2.ours_hbm
  67.4 2.3 %collective-permute-start.8 = (bf16[4,640,256]{2,1,0:T(8,128)(2,1)}, bf16[4,640,256]{2,1,0:T(8,128)(2,1)}, u32[]{:S(2)}, u32[]{:S(2)}) collective-permute-start(bf16[4,640,256]{2,1,0:T(8,128)(2,1)} %all-to-all-done.2.ours_hbm), channel_id=1, source_target_pairs={{0,8},{8,0},{16,24},{24,16},{32,40},{40,32},{48,56},{56,48},{64,72... | collective-permute-start | bytes 3932168 | tf_op jit(solution)/shard_map/ppermute | solution.py:260
  69.7 3.0 %collective-permute-done.8.theirs_hbm = bf16[4,640,256]{2,1,0:T(8,128)(2,1)} collective-permute-done((bf16[4,640,256]{2,1,0:T(8,128)(2,1)}, bf16[4,640,256]{2,1,0:T(8,128)(2,1)}, u32[]{:S(2)}, u32[]{:S(2)}) %collective-permute-start.8) | collective-permute-done | bytes 1310752 | tf_op jit(solution)/shard_map/ppermute | solution.py:260
  72.7 12.0 %shard_map.63 = (bf16[4,256,512]{2,1,0:T(8,128)(2,1)}, bf16[256,512]{1,0:T(8,128)(2,1)}) custom-call(s32[2]{0:T(128)} %pad_add_fusion.place_ref, bf16[1024,128]{1,0:T(8,128)(2,1)} %get-tuple-element.40.heads_ref.heads_hbm, f32[1024,256]{1,0:T(8,128)} %copy-done.1, f32[1024,128]{1,0:T(8,128)} %copy-done.5, bf16[4,640,256]{2,1,0:T(8,128)(2,1)} %all-to-all-done.2.ours_hbm, ...), custom_call_target="tpu_custom_call" | custom-call | flops 1048576 | bytes 65536 | tf_op jit(solution)/shard_map/pallas_call | solution.py:269
  84.7 0.0 copy-start.8
  84.8 0.0 copy-start.9
  84.8 4.2 %all-to-all-start.3 = ((bf16[4,256,512]{2,1,0:T(8,128)(2,1)}), bf16[4,256,512]{2,1,0:T(8,128)(2,1)S(1)}, u32[]{:S(2)}, u32[]{:S(2)}) async-start(bf16[4,256,512]{2,1,0:T(8,128)(2,1)} %get-tuple-element.57), calls=%async_computation.3 | async-start | bytes 2097152 | tf_op jit(solution)/shard_map/all_to_all | solution.py:285
  88.9 0.0 copy-done.8
  88.9 0.0 copy-done.9
  88.9 0.0 copy-start
  88.9 2.2 %copy-done = bf16[512,4096]{1,0:T(8,128)(2,1)S(1)} copy-done((bf16[512,4096]{1,0:T(8,128)(2,1)S(1)}, bf16[512,4096]{1,0:T(8,128)(2,1)}, u32[]{:S(2)}) %copy-start) | copy-done | bytes 4194328
  91.1 2.3 %shard_map.64 = bf16[4,256,512]{2,1,0:T(8,128)(2,1)} custom-call(s32[2]{0:T(128)S(1)} %copy-done.8, bf16[256,512]{1,0:T(8,128)(2,1)S(1)} %copy-done.9, bf16[512,4096]{1,0:T(8,128)(2,1)S(1)} %copy-done), custom_call_target="tpu_custom_call" | custom-call | flops 10000000000 | bytes 65536 | tf_op jit(solution)/shard_map/pallas_call | solution.py:269
  93.5 10.0 %all-to-all-done.3.parts_ref = bf16[4,256,512]{2,1,0:T(8,128)(2,1)S(1)} async-done(((bf16[4,256,512]{2,1,0:T(8,128)(2,1)}), bf16[4,256,512]{2,1,0:T(8,128)(2,1)S(1)}, u32[]{:S(2)}, u32[]{:S(2)}) %all-to-all-start.3) | async-done | bytes 1048608 | tf_op jit(solution)/shard_map/all_to_all | solution.py:285
  103.4 0.1 shard_map.65
  103.6 3.7 %collective-permute-start.9 = (bf16[256,512]{1,0:T(8,128)(2,1)S(1)}, bf16[256,512]{1,0:T(8,128)(2,1)S(1)}, u32[]{:S(2)}, u32[]{:S(2)}) collective-permute-start(bf16[256,512]{1,0:T(8,128)(2,1)S(1)} %shard_map.65), channel_id=1, source_target_pairs={{0,1},{1,0},{2,3},{3,2},{4,5},{5,4},{6,7},{7,6},{8,9},{9,8},{10,11... | collective-permute-start | bytes 786440 | tf_op jit(solution)/shard_map/ppermute | solution.py:399
  107.3 3.5 %all-to-all-start.4 = ((bf16[4,256,512]{2,1,0:T(8,128)(2,1)}), bf16[4,256,512]{2,1,0:T(8,128)(2,1)S(1)}, u32[]{:S(2)}, u32[]{:S(2)}) async-start(bf16[4,256,512]{2,1,0:T(8,128)(2,1)} %shard_map.64), calls=%async_computation.4 | async-start | bytes 2097152 | tf_op jit(solution)/shard_map/all_to_all | solution.py:285
  110.8 27.9 %collective-permute-done.9.value_ref = bf16[256,512]{1,0:T(8,128)(2,1)S(1)} collective-permute-done((bf16[256,512]{1,0:T(8,128)(2,1)S(1)}, bf16[256,512]{1,0:T(8,128)(2,1)S(1)}, u32[]{:S(2)}, u32[]{:S(2)}) %collective-permute-start.9) | collective-permute-done | bytes 262176 | tf_op jit(solution)/shard_map/ppermute | solution.py:399
  138.7 0.0 all-to-all-done.4.parts_ref
  138.8 0.9 shard_map.67
  (5 shorter events, 0.1 us)
Async XLA Ops:
  1.7 12.4 %collective-permute-start = (bf16[128,256]{1,0:T(8,128)(2,1)}, bf16[128,256]{1,0:T(8,128)(2,1)S(1)}, u32[]{:S(2)}, u32[]{:S(2)}) collective-permute-start(bf16[128,256]{1,0:T(8,128)(2,1)} %get-tuple-element.33.refs_0_), channel_id=1, source_target_pairs={{0,64},{8,72},{16,80},{24,88},{32,96},{40,104},{48,112},{56,120},{... | collective-permute-start | bytes 196616 | tf_op jit(solution)/shard_map/ppermute | solution.py:257
  6.9 1.3 collective-permute-start.1
  9.1 5.1 %copy-start.6 = (bf16[128,256]{1,0:T(8,128)(2,1)S(1)}, bf16[128,256]{1,0:T(8,128)(2,1)}, u32[]{:S(2)}) copy-start(bf16[128,256]{1,0:T(8,128)(2,1)} %get-tuple-element.33.refs_0_) | copy-start | bytes 196612
  14.2 7.6 %collective-permute-start.3 = (bf16[128,256]{1,0:T(8,128)(2,1)S(1)}, bf16[128,256]{1,0:T(8,128)(2,1)S(1)}, u32[]{:S(2)}, u32[]{:S(2)}) collective-permute-start(bf16[128,256]{1,0:T(8,128)(2,1)S(1)} %broadcast_select_fusion.2), channel_id=1, source_target_pairs={{0,32},{64,96},{1,33},{65,97},{2,34},{66,98},{3,35},{67,99},{4,36}... | collective-permute-start | bytes 196616 | tf_op jit(solution)/shard_map/ppermute | solution.py:281
  14.9 6.9 %collective-permute-start.2 = (bf16[256,256]{1,0:T(8,128)(2,1)S(1)}, bf16[256,256]{1,0:T(8,128)(2,1)S(1)}, u32[]{:S(2)}, u32[]{:S(2)}) collective-permute-start(bf16[256,256]{1,0:T(8,128)(2,1)S(1)} %shard_map.57.refs_0_), channel_id=1, source_target_pairs={{0,32},{8,40},{16,48},{24,56},{32,0},{40,8},{48,16},{56,24},{64,96... | collective-permute-start | bytes 393224 | tf_op jit(solution)/shard_map/ppermute | solution.py:257
  17.6 12.9 %all-to-all-start = ((bf16[4,256,256]{2,1,0:T(8,128)(2,1)}), bf16[4,256,256]{2,1,0:T(8,128)(2,1)S(1)}, u32[]{:S(2)}, u32[]{:S(2)}) async-start(bf16[4,256,256]{2,1,0:T(8,128)(2,1)} %shard_map.58), calls=%async_computation | async-start | bytes 1048576 | tf_op jit(solution)/shard_map/all_to_all | solution.py:264
  21.8 8.7 %collective-permute-start.5 = (bf16[128,256]{1,0:T(8,128)(2,1)S(1)}, bf16[128,256]{1,0:T(8,128)(2,1)S(1)}, u32[]{:S(2)}, u32[]{:S(2)}) collective-permute-start(bf16[128,256]{1,0:T(8,128)(2,1)S(1)} %broadcast_select_fusion.1), channel_id=1, source_target_pairs={{0,16},{32,48},{64,80},{96,112},{1,17},{33,49},{65,81},{97,113},{2... | collective-permute-start | bytes 196616 | tf_op jit(solution)/shard_map/ppermute | solution.py:281
  22.5 21.9 %collective-permute-start.4 = (bf16[512,256]{1,0:T(8,128)(2,1)S(1)}, bf16[512,256]{1,0:T(8,128)(2,1)S(1)}, u32[]{:S(2)}, u32[]{:S(2)}) collective-permute-start(bf16[512,256]{1,0:T(8,128)(2,1)S(1)} %shard_map.60), channel_id=1, source_target_pairs={{0,16},{8,24},{16,0},{24,8},{32,48},{40,56},{48,32},{56,40},{64,80... | collective-permute-start | bytes 786440 | tf_op jit(solution)/shard_map/ppermute | solution.py:257
  30.5 15.1 %all-to-all-start.1 = ((bf16[4,256,256]{2,1,0:T(8,128)(2,1)}), bf16[4,256,256]{2,1,0:T(8,128)(2,1)S(1)}, u32[]{:S(2)}, u32[]{:S(2)}) async-start(bf16[4,256,256]{2,1,0:T(8,128)(2,1)} %shard_map.59), calls=%async_computation.1 | async-start | bytes 1048576 | tf_op jit(solution)/shard_map/all_to_all | solution.py:264
  34.7 11.3 %collective-permute-start.6 = (bf16[4,256,256]{2,1,0:T(8,128)(2,1)S(1)}, bf16[4,256,256]{2,1,0:T(8,128)(2,1)S(1)}, u32[]{:S(2)}, u32[]{:S(2)}) collective-permute-start(bf16[4,256,256]{2,1,0:T(8,128)(2,1)S(1)} %all-to-all-done.two_ref), channel_id=1, source_target_pairs={{0,8},{8,0},{16,24},{24,16},{32,40},{40,32},{48,56},{56,48},{64,72... | collective-permute-start | bytes 1572872 | tf_op jit(solution)/shard_map/ppermute | solution.py:260
  45.6 12.7 %copy-start.2 = (bf16[1024,128]{1,0:T(8,128)(2,1)S(1)}, bf16[1024,128]{1,0:T(8,128)(2,1)}, u32[]{:S(2)}) copy-start(bf16[1024,128]{1,0:T(8,128)(2,1)} %get-tuple-element.40.heads_ref.heads_hbm) | copy-start | bytes 786436
  45.6 12.7 %copy-start.3 = (f32[1024,256]{1,0:T(8,128)S(1)}, f32[1024,256]{1,0:T(8,128)}, u32[]{:S(2)}) copy-start(f32[1024,256]{1,0:T(8,128)} %get-tuple-element.48.acc_in) | copy-start | bytes 3145732
  45.6 12.7 %copy-start.4 = (f32[1024,128]{1,0:T(8,128)S(1)}, f32[1024,128]{1,0:T(8,128)}, u32[]{:S(2)}) copy-start(f32[1024,128]{1,0:T(8,128)} %get-tuple-element.49.top_in) | copy-start | bytes 1572868
  45.6 12.7 %copy-start.7 = (s32[2]{0:T(128)S(1)}, s32[2]{0:T(128)}, u32[]{:S(2)}) copy-start(s32[2]{0:T(128)} %pad_add_fusion.place_ref) | copy-start | bytes 28
  45.9 21.5 %all-to-all-start.2 = ((bf16[4,640,256]{2,1,0:T(8,128)(2,1)}), bf16[4,640,256]{2,1,0:T(8,128)(2,1)}, u32[]{:S(2)}, u32[]{:S(2)}) async-start(bf16[4,640,256]{2,1,0:T(8,128)(2,1)} %shard_map.61), calls=%async_computation.2 | async-start | bytes 2621440 | tf_op jit(solution)/shard_map/all_to_all | solution.py:264
  50.4 7.9 %collective-permute-start.7 = (bf16[4,256,256]{2,1,0:T(8,128)(2,1)S(1)}, bf16[4,256,256]{2,1,0:T(8,128)(2,1)S(1)}, u32[]{:S(2)}, u32[]{:S(2)}) collective-permute-start(bf16[4,256,256]{2,1,0:T(8,128)(2,1)S(1)} %all-to-all-done.1.pair_ref), channel_id=1, source_target_pairs={{0,8},{8,0},{16,24},{24,16},{32,40},{40,32},{48,56},{56,48},{64,72... | collective-permute-start | bytes 1572872 | tf_op jit(solution)/shard_map/ppermute | solution.py:260
  65.7 1.0 copy-start.1
  66.6 0.8 copy-start.5
  67.4 5.3 %collective-permute-start.8 = (bf16[4,640,256]{2,1,0:T(8,128)(2,1)}, bf16[4,640,256]{2,1,0:T(8,128)(2,1)}, u32[]{:S(2)}, u32[]{:S(2)}) collective-permute-start(bf16[4,640,256]{2,1,0:T(8,128)(2,1)} %all-to-all-done.2.ours_hbm), channel_id=1, source_target_pairs={{0,8},{8,0},{16,24},{24,16},{32,40},{40,32},{48,56},{56,48},{64,72... | collective-permute-start | bytes 3932168 | tf_op jit(solution)/shard_map/ppermute | solution.py:260
  84.7 4.2 %copy-start.8 = (s32[2]{0:T(128)S(1)}, s32[2]{0:T(128)}, u32[]{:S(2)}) copy-start(s32[2]{0:T(128)} %pad_add_fusion.place_ref) | copy-start | bytes 28
  84.8 4.2 %copy-start.9 = (bf16[256,512]{1,0:T(8,128)(2,1)S(1)}, bf16[256,512]{1,0:T(8,128)(2,1)}, u32[]{:S(2)}) copy-start(bf16[256,512]{1,0:T(8,128)(2,1)} %get-tuple-element.58.rows_hbm) | copy-start | bytes 786436
  84.8 18.7 %all-to-all-start.3 = ((bf16[4,256,512]{2,1,0:T(8,128)(2,1)}), bf16[4,256,512]{2,1,0:T(8,128)(2,1)S(1)}, u32[]{:S(2)}, u32[]{:S(2)}) async-start(bf16[4,256,512]{2,1,0:T(8,128)(2,1)} %get-tuple-element.57), calls=%async_computation.3 | async-start | bytes 2097152 | tf_op jit(solution)/shard_map/all_to_all | solution.py:285
  88.9 2.2 %copy-start = (bf16[512,4096]{1,0:T(8,128)(2,1)S(1)}, bf16[512,4096]{1,0:T(8,128)(2,1)}, u32[]{:S(2)}) copy-start(bf16[512,4096]{1,0:T(8,128)(2,1)} %weight_hbm.3) | copy-start | bytes 12582916
  103.6 35.1 %collective-permute-start.9 = (bf16[256,512]{1,0:T(8,128)(2,1)S(1)}, bf16[256,512]{1,0:T(8,128)(2,1)S(1)}, u32[]{:S(2)}, u32[]{:S(2)}) collective-permute-start(bf16[256,512]{1,0:T(8,128)(2,1)S(1)} %shard_map.65), channel_id=1, source_target_pairs={{0,1},{1,0},{2,3},{3,2},{4,5},{5,4},{6,7},{7,6},{8,9},{9,8},{10,11... | collective-permute-start | bytes 786440 | tf_op jit(solution)/shard_map/ppermute | solution.py:399
  107.3 31.4 %all-to-all-start.4 = ((bf16[4,256,512]{2,1,0:T(8,128)(2,1)}), bf16[4,256,512]{2,1,0:T(8,128)(2,1)S(1)}, u32[]{:S(2)}, u32[]{:S(2)}) async-start(bf16[4,256,512]{2,1,0:T(8,128)(2,1)} %shard_map.64), calls=%async_computation.4 | async-start | bytes 2097152 | tf_op jit(solution)/shard_map/all_to_all | solution.py:285
